TPU v7x, 512 devices: a whole 4x8x8 slice. The times are simulated.
512 devices in a mesh: ctx: 16 (over y, z_lo), kvh: 8 (over x, core), rep: 4 (over z_hi).
Axes of the slice: x: 4, y: 8, z: 8 (z_hi: 4, z_lo: 2; z = z_hi * 2 + z_lo), core: 2. Of those that a mesh axis runs over, the one named last changes fastest.
Arguments:
- queries: bfloat16 [256, 128, 128], P(('ctx', 'rep'), 'kvh'), may hold values from -5 to 5
- prompt_keys: bfloat16 [65536, 8, 128], P('ctx', 'kvh'), may hold values from -5 to 5
- prompt_values: bfloat16 [65536, 8, 128], P('ctx', 'kvh'), may hold values from -2.5 to 2.5
- suffix_keys: bfloat16 [256, 512, 8, 128], P(('ctx', 'rep'), None, 'kvh'), may hold values from -10 to 10
- suffix_values: bfloat16 [256, 512, 8, 128], P(('ctx', 'rep'), None, 'kvh'), may hold values from -2.5 to 2.5
- suffix_len: int32 [256], P(('ctx', 'rep')), may hold values from 0 to 512, as said below
- out_weight: bfloat16 [16384, 16384], P('kvh', ('ctx', 'rep')), may hold values from -0.046875 to 0.046875
Outputs:
- attended: bfloat16 [256, 128, 128], P(('ctx', 'rep'), 'kvh')
- projected: bfloat16 [256, 16384], P('kvh', ('ctx', 'rep'))
Inputs may be any that keep to these rules, and one draw needn't show every extreme that they name: `suffix_len`: some continuation has 512 live private positions and some has none.
All inputs are finite; a program needn't handle non-finite values.
Results may differ from a plain program's by a relative error of at most 0.015.
Values may be sent and summed in bfloat16 or wider, within the bound.
No kernel may reach another device: no remote copies, remote signals or barrier semaphores. Data moves between devices by JAX's collectives and lax.ppermute only.
A program may use at most 64 MiB of HBM per device.

v0:
```python
import math

import jax
import jax.numpy as jnp
from jax import lax
from jax.sharding import PartitionSpec as P

FAR_BELOW = -1e30


def passed_along(value, axis, steps):
    count = lax.axis_size(axis)
    pairs = [(source, (source + steps) % count) for source in range(count)]
    return lax.ppermute(value, axis, pairs)


def partial_state(query_rows, key_block, value_block, factor):
    scores = (
        lax.dot_general(
            query_rows, key_block, (((1,), (1,)), ((), ())), preferred_element_type=jnp.float32
        )
        * factor
    )
    highest = jnp.max(scores, axis=1)
    weights = jnp.exp(scores - highest[:, None])
    totals = jnp.sum(weights, axis=1)
    numer = jnp.dot(weights.astype(jnp.bfloat16), value_block, preferred_element_type=jnp.float32)
    return (numer, highest, totals)


def combine_states(first_state, second_state):
    numer_one, highest_one, totals_one = first_state
    numer_two, highest_two, totals_two = second_state
    joint = jnp.maximum(highest_one, highest_two)
    weight_one = jnp.exp(highest_one - joint)
    weight_two = jnp.exp(highest_two - joint)
    numer = numer_one * weight_one[:, None] + numer_two * weight_two[:, None]
    return (numer, joint, totals_one * weight_one + totals_two * weight_two)


def suffix_state(queries, suffix_keys, suffix_values, suffix_len, factor):
    cont_local, heads_local, head_dim = queries.shape
    key_set = suffix_keys[:, :, 0, :]
    value_set = suffix_values[:, :, 0, :]
    scores = (
        jnp.einsum("cqd,cud->cqu", queries, key_set, preferred_element_type=jnp.float32) * factor
    )
    live = lax.broadcasted_iota(jnp.int32, scores.shape, 2) < suffix_len[:, None, None]
    scores = jnp.where(live, scores, FAR_BELOW)
    highest = jnp.max(scores, axis=2)
    weights = jnp.where(live, jnp.exp(scores - highest[:, :, None]), 0.0)
    totals = jnp.sum(weights, axis=2)
    numer = jnp.einsum(
        "cqu,cud->cqd", weights.astype(jnp.bfloat16), value_set, preferred_element_type=jnp.float32
    )
    rows = cont_local * heads_local
    return (numer.reshape(rows, head_dim), highest.reshape(rows), totals.reshape(rows))


def body(queries, prompt_keys, prompt_values, suffix_keys, suffix_values, suffix_len, out_weight):
    cont_local, heads_local, head_dim = queries.shape
    factor = 1.0 / math.sqrt(head_dim)
    rows = cont_local * heads_local
    query_rows = queries.reshape(rows, head_dim)
    key_block = prompt_keys[:, 0, :]
    value_block = prompt_values[:, 0, :]
    home_state = suffix_state(queries, suffix_keys, suffix_values, suffix_len, factor)
    cycle_width = lax.axis_size("ctx")

    def advance(turn_index, carried):
        visiting, numer, highest, totals = carried
        local_state = partial_state(visiting, key_block, value_block, factor)
        numer, highest, totals = combine_states((numer, highest, totals), local_state)
        visiting = passed_along(visiting, "ctx", 1)
        numer, highest, totals = passed_along((numer, highest, totals), "ctx", 1)
        return (visiting, numer, highest, totals)

    final_carry = lax.fori_loop(0, cycle_width, advance, (query_rows,) + home_state)
    numer, totals = (final_carry[1], final_carry[3])
    attended = (numer / totals[:, None]).astype(jnp.bfloat16)
    attended_heads = attended.reshape(cont_local, heads_local, head_dim)
    flat_rows = attended.reshape(cont_local, heads_local * head_dim)
    terms = jnp.dot(
        lax.all_gather(flat_rows, ("ctx", "rep"), axis=0, tiled=True),
        out_weight,
        preferred_element_type=jnp.float32,
    )
    projected = lax.psum_scatter(terms, "kvh", scatter_dimension=0, tiled=True).astype(jnp.bfloat16)
    return (attended_heads, projected)


def solution(mesh):
    in_specs = (
        P(("ctx", "rep"), "kvh", None),
        P("ctx", "kvh", None),
        P("ctx", "kvh", None),
        P(("ctx", "rep"), None, "kvh", None),
        P(("ctx", "rep"), None, "kvh", None),
        P(("ctx", "rep")),
        P("kvh", ("ctx", "rep")),
    )
    out_specs = (P(("ctx", "rep"), "kvh", None), P("kvh", ("ctx", "rep")))
    return jax.shard_map(body, mesh=mesh, in_specs=in_specs, out_specs=out_specs, check_vma=False)
```

profile of v0, /device:TPU:1, one launch (start us, length us, event | category | flops | bytes accessed | tf_op | source)
XLA Modules:
  0.0 623.4 jit_solution(3487838340445731764)
XLA Ops:
  11.8 262.4 %while.16 = (s32[]{:T(128)}, bf16[64,128]{1,0:T(8,128)(2,1)S(1)}, f32[64,128]{1,0:T(8,128)S(1)}, f32[64]{0:T(128)S(1)}, f32[64]{0:T(128)S(1)}, /*index=5*/bf16[4...) while((s32[]{:T(128)}, bf16[64,128]{1,0:T(8,128)(2,1)S(1)}, f32[64,128]{1,0:T(8,128)S(1)}, ...), condition=%wide.region_5.6_spmd, body=%wide.region_2.5_spmd.sunk | while | flops 135815424 | bytes 9754385 | solution.py:78
  14.0 4.8 collective-permute-start.1
  21.1 4.0 collective-permute-start.2
  27.5 4.0 collective-permute-done.3
  35.7 3.2 collective-permute-start
  40.8 4.4 collective-permute-start.3
  51.7 3.9 collective-permute-start
  55.6 3.6 collective-permute-start.2
  59.2 3.0 collective-permute-start.3
  62.2 3.3 collective-permute-done.3
  69.7 3.5 collective-permute-start
  75.1 2.8 collective-permute-start.3
  104.7 4.1 collective-permute-start.3
  115.2 4.0 collective-permute-start
  121.2 3.1 collective-permute-start.3
  131.7 3.5 collective-permute-start
  135.2 3.0 collective-permute-start.2
  138.3 4.5 collective-permute-start.3
  149.2 4.0 collective-permute-start
  155.2 3.8 collective-permute-start.3
  165.8 4.1 collective-permute-start
  200.7 4.3 collective-permute-start.3
  211.6 3.7 collective-permute-start
  217.4 4.5 collective-permute-start.3
  228.3 4.5 collective-permute-start
  234.8 4.0 collective-permute-start.3
  245.3 4.0 collective-permute-start
  251.3 4.0 collective-permute-start.3
  262.1 3.8 collective-permute-start
  267.8 2.8 collective-permute-start.3
  275.0 261.7 %all-gather.3.cloned.1.call-done = bf16[64,4,2048]{2,1,0:T(4,128)(2,1)} async-done(((bf16[1,4,2048]{2,1,0:T(4,128)(2,1)}), bf16[64,4,2048]{2,1,0:T(4,128)(2,1)}) %all-gather.3.cloned.1.call-update) | async-done | bytes 1048592 | tf_op jit(solution)/shard_map/all_gather | solution.py:84
  539.2 75.9 %reduce-scatter.2.cloned.1.call-done = f32[32,256]{1,0:T(8,128)} async-done(((f32[256,256]{1,0:T(8,128)}), f32[32,256]{1,0:T(8,128)}) %reduce-scatter.2.cloned.1.call-update) | async-done | bytes 32784 | tf_op jit(solution)/shard_map/reduce_scatter | solution.py:88
  (232 shorter events, 160.3 us)
Async XLA Ops:
  7.2 529.5 %all-gather.3.cloned.1.call-start = ((), (), s32[]{:S(2)}) async-start(), calls=%async_computation.2 | async-start | bytes 1064960 | tf_op jit(solution)/shard_map/all_gather | solution.py:84
  14.0 17.5 %collective-permute-start.1 = (f32[64,128]{1,0:T(8,128)S(1)}, f32[64,128]{1,0:T(8,128)S(1)}, u32[]{:S(2)}, u32[]{:S(2)}) collective-permute-start(f32[64,128]{1,0:T(8,128)S(1)} %fusion.38), channel_id=1, source_target_pairs={{0,32},{32,64},{64,96},{96,128},{128,160},{160,192},{192,224},{224... | collective-permute-start | bytes 98312 | tf_op jit(solution)/shard_map/while/body/eval_jaxpr/ppermute | solution.py:14
  18.8 12.7 %collective-permute-start = (bf16[64,128]{1,0:T(8,128)(2,1)S(1)}, bf16[64,128]{1,0:T(8,128)(2,1)S(1)}, u32[]{:S(2)}, u32[]{:S(2)}) collective-permute-start(bf16[64,128]{1,0:T(8,128)(2,1)S(1)} %copy.15), channel_id=1, source_target_pairs={{0,32},{32,64},{64,96},{96,128},{128,160},{160,192},{192,224},{224... | collective-permute-start | bytes 49160 | tf_op jit(solution)/shard_map/while/body/eval_jaxpr/ppermute | solution.py:14
  33.7 13.4 %collective-permute-start.1 = (f32[64,128]{1,0:T(8,128)S(1)}, f32[64,128]{1,0:T(8,128)S(1)}, u32[]{:S(2)}, u32[]{:S(2)}) collective-permute-start(f32[64,128]{1,0:T(8,128)S(1)} %fusion.38), channel_id=1, source_target_pairs={{0,32},{32,64},{64,96},{96,128},{128,160},{160,192},{192,224},{224... | collective-permute-start | bytes 98312 | tf_op jit(solution)/shard_map/while/body/eval_jaxpr/ppermute | solution.py:14
  35.7 11.5 %collective-permute-start = (bf16[64,128]{1,0:T(8,128)(2,1)S(1)}, bf16[64,128]{1,0:T(8,128)(2,1)S(1)}, u32[]{:S(2)}, u32[]{:S(2)}) collective-permute-start(bf16[64,128]{1,0:T(8,128)(2,1)S(1)} %copy.15), channel_id=1, source_target_pairs={{0,32},{32,64},{64,96},{96,128},{128,160},{160,192},{192,224},{224... | collective-permute-start | bytes 49160 | tf_op jit(solution)/shard_map/while/body/eval_jaxpr/ppermute | solution.py:14
  49.4 16.2 %collective-permute-start.1 = (f32[64,128]{1,0:T(8,128)S(1)}, f32[64,128]{1,0:T(8,128)S(1)}, u32[]{:S(2)}, u32[]{:S(2)}) collective-permute-start(f32[64,128]{1,0:T(8,128)S(1)} %fusion.38), channel_id=1, source_target_pairs={{0,32},{32,64},{64,96},{96,128},{128,160},{160,192},{192,224},{224... | collective-permute-start | bytes 98312 | tf_op jit(solution)/shard_map/while/body/eval_jaxpr/ppermute | solution.py:14
  51.7 13.9 %collective-permute-start = (bf16[64,128]{1,0:T(8,128)(2,1)S(1)}, bf16[64,128]{1,0:T(8,128)(2,1)S(1)}, u32[]{:S(2)}, u32[]{:S(2)}) collective-permute-start(bf16[64,128]{1,0:T(8,128)(2,1)S(1)} %copy.15), channel_id=1, source_target_pairs={{0,32},{32,64},{64,96},{96,128},{128,160},{160,192},{192,224},{224... | collective-permute-start | bytes 49160 | tf_op jit(solution)/shard_map/while/body/eval_jaxpr/ppermute | solution.py:14
  67.8 14.0 %collective-permute-start.1 = (f32[64,128]{1,0:T(8,128)S(1)}, f32[64,128]{1,0:T(8,128)S(1)}, u32[]{:S(2)}, u32[]{:S(2)}) collective-permute-start(f32[64,128]{1,0:T(8,128)S(1)} %fusion.38), channel_id=1, source_target_pairs={{0,32},{32,64},{64,96},{96,128},{128,160},{160,192},{192,224},{224... | collective-permute-start | bytes 98312 | tf_op jit(solution)/shard_map/while/body/eval_jaxpr/ppermute | solution.py:14
  69.7 12.1 %collective-permute-start = (bf16[64,128]{1,0:T(8,128)(2,1)S(1)}, bf16[64,128]{1,0:T(8,128)(2,1)S(1)}, u32[]{:S(2)}, u32[]{:S(2)}) collective-permute-start(bf16[64,128]{1,0:T(8,128)(2,1)S(1)} %copy.15), channel_id=1, source_target_pairs={{0,32},{32,64},{64,96},{96,128},{128,160},{160,192},{192,224},{224... | collective-permute-start | bytes 49160 | tf_op jit(solution)/shard_map/while/body/eval_jaxpr/ppermute | solution.py:14
  84.0 12.6 %collective-permute-start.1 = (f32[64,128]{1,0:T(8,128)S(1)}, f32[64,128]{1,0:T(8,128)S(1)}, u32[]{:S(2)}, u32[]{:S(2)}) collective-permute-start(f32[64,128]{1,0:T(8,128)S(1)} %fusion.38), channel_id=1, source_target_pairs={{0,32},{32,64},{64,96},{96,128},{128,160},{160,192},{192,224},{224... | collective-permute-start | bytes 98312 | tf_op jit(solution)/shard_map/while/body/eval_jaxpr/ppermute | solution.py:14
  86.0 10.7 %collective-permute-start = (bf16[64,128]{1,0:T(8,128)(2,1)S(1)}, bf16[64,128]{1,0:T(8,128)(2,1)S(1)}, u32[]{:S(2)}, u32[]{:S(2)}) collective-permute-start(bf16[64,128]{1,0:T(8,128)(2,1)S(1)} %copy.15), channel_id=1, source_target_pairs={{0,32},{32,64},{64,96},{96,128},{128,160},{160,192},{192,224},{224... | collective-permute-start | bytes 49160 | tf_op jit(solution)/shard_map/while/body/eval_jaxpr/ppermute | solution.py:14
  98.9 12.2 %collective-permute-start.1 = (f32[64,128]{1,0:T(8,128)S(1)}, f32[64,128]{1,0:T(8,128)S(1)}, u32[]{:S(2)}, u32[]{:S(2)}) collective-permute-start(f32[64,128]{1,0:T(8,128)S(1)} %fusion.38), channel_id=1, source_target_pairs={{0,32},{32,64},{64,96},{96,128},{128,160},{160,192},{192,224},{224... | collective-permute-start | bytes 98312 | tf_op jit(solution)/shard_map/while/body/eval_jaxpr/ppermute | solution.py:14
  113.3 14.3 %collective-permute-start.1 = (f32[64,128]{1,0:T(8,128)S(1)}, f32[64,128]{1,0:T(8,128)S(1)}, u32[]{:S(2)}, u32[]{:S(2)}) collective-permute-start(f32[64,128]{1,0:T(8,128)S(1)} %fusion.38), channel_id=1, source_target_pairs={{0,32},{32,64},{64,96},{96,128},{128,160},{160,192},{192,224},{224... | collective-permute-start | bytes 98312 | tf_op jit(solution)/shard_map/while/body/eval_jaxpr/ppermute | solution.py:14
  115.2 12.4 %collective-permute-start = (bf16[64,128]{1,0:T(8,128)(2,1)S(1)}, bf16[64,128]{1,0:T(8,128)(2,1)S(1)}, u32[]{:S(2)}, u32[]{:S(2)}) collective-permute-start(bf16[64,128]{1,0:T(8,128)(2,1)S(1)} %copy.15), channel_id=1, source_target_pairs={{0,32},{32,64},{64,96},{96,128},{128,160},{160,192},{192,224},{224... | collective-permute-start | bytes 49160 | tf_op jit(solution)/shard_map/while/body/eval_jaxpr/ppermute | solution.py:14
  129.8 14.9 %collective-permute-start.1 = (f32[64,128]{1,0:T(8,128)S(1)}, f32[64,128]{1,0:T(8,128)S(1)}, u32[]{:S(2)}, u32[]{:S(2)}) collective-permute-start(f32[64,128]{1,0:T(8,128)S(1)} %fusion.38), channel_id=1, source_target_pairs={{0,32},{32,64},{64,96},{96,128},{128,160},{160,192},{192,224},{224... | collective-permute-start | bytes 98312 | tf_op jit(solution)/shard_map/while/body/eval_jaxpr/ppermute | solution.py:14
  131.7 13.0 %collective-permute-start = (bf16[64,128]{1,0:T(8,128)(2,1)S(1)}, bf16[64,128]{1,0:T(8,128)(2,1)S(1)}, u32[]{:S(2)}, u32[]{:S(2)}) collective-permute-start(bf16[64,128]{1,0:T(8,128)(2,1)S(1)} %copy.15), channel_id=1, source_target_pairs={{0,32},{32,64},{64,96},{96,128},{128,160},{160,192},{192,224},{224... | collective-permute-start | bytes 49160 | tf_op jit(solution)/shard_map/while/body/eval_jaxpr/ppermute | solution.py:14
  146.9 14.8 %collective-permute-start.1 = (f32[64,128]{1,0:T(8,128)S(1)}, f32[64,128]{1,0:T(8,128)S(1)}, u32[]{:S(2)}, u32[]{:S(2)}) collective-permute-start(f32[64,128]{1,0:T(8,128)S(1)} %fusion.38), channel_id=1, source_target_pairs={{0,32},{32,64},{64,96},{96,128},{128,160},{160,192},{192,224},{224... | collective-permute-start | bytes 98312 | tf_op jit(solution)/shard_map/while/body/eval_jaxpr/ppermute | solution.py:14
  149.2 12.4 %collective-permute-start = (bf16[64,128]{1,0:T(8,128)(2,1)S(1)}, bf16[64,128]{1,0:T(8,128)(2,1)S(1)}, u32[]{:S(2)}, u32[]{:S(2)}) collective-permute-start(bf16[64,128]{1,0:T(8,128)(2,1)S(1)} %copy.15), channel_id=1, source_target_pairs={{0,32},{32,64},{64,96},{96,128},{128,160},{160,192},{192,224},{224... | collective-permute-start | bytes 49160 | tf_op jit(solution)/shard_map/while/body/eval_jaxpr/ppermute | solution.py:14
  163.8 14.3 %collective-permute-start.1 = (f32[64,128]{1,0:T(8,128)S(1)}, f32[64,128]{1,0:T(8,128)S(1)}, u32[]{:S(2)}, u32[]{:S(2)}) collective-permute-start(f32[64,128]{1,0:T(8,128)S(1)} %fusion.38), channel_id=1, source_target_pairs={{0,32},{32,64},{64,96},{96,128},{128,160},{160,192},{192,224},{224... | collective-permute-start | bytes 98312 | tf_op jit(solution)/shard_map/while/body/eval_jaxpr/ppermute | solution.py:14
  165.8 12.4 %collective-permute-start = (bf16[64,128]{1,0:T(8,128)(2,1)S(1)}, bf16[64,128]{1,0:T(8,128)(2,1)S(1)}, u32[]{:S(2)}, u32[]{:S(2)}) collective-permute-start(bf16[64,128]{1,0:T(8,128)(2,1)S(1)} %copy.15), channel_id=1, source_target_pairs={{0,32},{32,64},{64,96},{96,128},{128,160},{160,192},{192,224},{224... | collective-permute-start | bytes 49160 | tf_op jit(solution)/shard_map/while/body/eval_jaxpr/ppermute | solution.py:14
  180.4 12.4 %collective-permute-start.1 = (f32[64,128]{1,0:T(8,128)S(1)}, f32[64,128]{1,0:T(8,128)S(1)}, u32[]{:S(2)}, u32[]{:S(2)}) collective-permute-start(f32[64,128]{1,0:T(8,128)S(1)} %fusion.38), channel_id=1, source_target_pairs={{0,32},{32,64},{64,96},{96,128},{128,160},{160,192},{192,224},{224... | collective-permute-start | bytes 98312 | tf_op jit(solution)/shard_map/while/body/eval_jaxpr/ppermute | solution.py:14
  182.3 10.4 %collective-permute-start = (bf16[64,128]{1,0:T(8,128)(2,1)S(1)}, bf16[64,128]{1,0:T(8,128)(2,1)S(1)}, u32[]{:S(2)}, u32[]{:S(2)}) collective-permute-start(bf16[64,128]{1,0:T(8,128)(2,1)S(1)} %copy.15), channel_id=1, source_target_pairs={{0,32},{32,64},{64,96},{96,128},{128,160},{160,192},{192,224},{224... | collective-permute-start | bytes 49160 | tf_op jit(solution)/shard_map/while/body/eval_jaxpr/ppermute | solution.py:14
  194.9 12.2 %collective-permute-start.1 = (f32[64,128]{1,0:T(8,128)S(1)}, f32[64,128]{1,0:T(8,128)S(1)}, u32[]{:S(2)}, u32[]{:S(2)}) collective-permute-start(f32[64,128]{1,0:T(8,128)S(1)} %fusion.38), channel_id=1, source_target_pairs={{0,32},{32,64},{64,96},{96,128},{128,160},{160,192},{192,224},{224... | collective-permute-start | bytes 98312 | tf_op jit(solution)/shard_map/while/body/eval_jaxpr/ppermute | solution.py:14
  209.3 14.4 %collective-permute-start.1 = (f32[64,128]{1,0:T(8,128)S(1)}, f32[64,128]{1,0:T(8,128)S(1)}, u32[]{:S(2)}, u32[]{:S(2)}) collective-permute-start(f32[64,128]{1,0:T(8,128)S(1)} %fusion.38), channel_id=1, source_target_pairs={{0,32},{32,64},{64,96},{96,128},{128,160},{160,192},{192,224},{224... | collective-permute-start | bytes 98312 | tf_op jit(solution)/shard_map/while/body/eval_jaxpr/ppermute | solution.py:14
  211.6 12.2 %collective-permute-start = (bf16[64,128]{1,0:T(8,128)(2,1)S(1)}, bf16[64,128]{1,0:T(8,128)(2,1)S(1)}, u32[]{:S(2)}, u32[]{:S(2)}) collective-permute-start(bf16[64,128]{1,0:T(8,128)(2,1)S(1)} %copy.15), channel_id=1, source_target_pairs={{0,32},{32,64},{64,96},{96,128},{128,160},{160,192},{192,224},{224... | collective-permute-start | bytes 49160 | tf_op jit(solution)/shard_map/while/body/eval_jaxpr/ppermute | solution.py:14
  226.0 15.2 %collective-permute-start.1 = (f32[64,128]{1,0:T(8,128)S(1)}, f32[64,128]{1,0:T(8,128)S(1)}, u32[]{:S(2)}, u32[]{:S(2)}) collective-permute-start(f32[64,128]{1,0:T(8,128)S(1)} %fusion.38), channel_id=1, source_target_pairs={{0,32},{32,64},{64,96},{96,128},{128,160},{160,192},{192,224},{224... | collective-permute-start | bytes 98312 | tf_op jit(solution)/shard_map/while/body/eval_jaxpr/ppermute | solution.py:14
  228.3 12.8 %collective-permute-start = (bf16[64,128]{1,0:T(8,128)(2,1)S(1)}, bf16[64,128]{1,0:T(8,128)(2,1)S(1)}, u32[]{:S(2)}, u32[]{:S(2)}) collective-permute-start(bf16[64,128]{1,0:T(8,128)(2,1)S(1)} %copy.15), channel_id=1, source_target_pairs={{0,32},{32,64},{64,96},{96,128},{128,160},{160,192},{192,224},{224... | collective-permute-start | bytes 49160 | tf_op jit(solution)/shard_map/while/body/eval_jaxpr/ppermute | solution.py:14
  243.4 14.4 %collective-permute-start.1 = (f32[64,128]{1,0:T(8,128)S(1)}, f32[64,128]{1,0:T(8,128)S(1)}, u32[]{:S(2)}, u32[]{:S(2)}) collective-permute-start(f32[64,128]{1,0:T(8,128)S(1)} %fusion.38), channel_id=1, source_target_pairs={{0,32},{32,64},{64,96},{96,128},{128,160},{160,192},{192,224},{224... | collective-permute-start | bytes 98312 | tf_op jit(solution)/shard_map/while/body/eval_jaxpr/ppermute | solution.py:14
  245.3 12.4 %collective-permute-start = (bf16[64,128]{1,0:T(8,128)(2,1)S(1)}, bf16[64,128]{1,0:T(8,128)(2,1)S(1)}, u32[]{:S(2)}, u32[]{:S(2)}) collective-permute-start(bf16[64,128]{1,0:T(8,128)(2,1)S(1)} %copy.15), channel_id=1, source_target_pairs={{0,32},{32,64},{64,96},{96,128},{128,160},{160,192},{192,224},{224... | collective-permute-start | bytes 49160 | tf_op jit(solution)/shard_map/while/body/eval_jaxpr/ppermute | solution.py:14
  259.9 14.3 %collective-permute-start.1 = (f32[64,128]{1,0:T(8,128)S(1)}, f32[64,128]{1,0:T(8,128)S(1)}, u32[]{:S(2)}, u32[]{:S(2)}) collective-permute-start(f32[64,128]{1,0:T(8,128)S(1)} %fusion.38), channel_id=1, source_target_pairs={{0,32},{32,64},{64,96},{96,128},{128,160},{160,192},{192,224},{224... | collective-permute-start | bytes 98312 | tf_op jit(solution)/shard_map/while/body/eval_jaxpr/ppermute | solution.py:14
  262.1 12.1 %collective-permute-start = (bf16[64,128]{1,0:T(8,128)(2,1)S(1)}, bf16[64,128]{1,0:T(8,128)(2,1)S(1)}, u32[]{:S(2)}, u32[]{:S(2)}) collective-permute-start(bf16[64,128]{1,0:T(8,128)(2,1)S(1)} %copy.15), channel_id=1, source_target_pairs={{0,32},{32,64},{64,96},{96,128},{128,160},{160,192},{192,224},{224... | collective-permute-start | bytes 49160 | tf_op jit(solution)/shard_map/while/body/eval_jaxpr/ppermute | solution.py:14
  275.0 340.2 %reduce-scatter.2.cloned.1.call-start = ((), (), s32[]{:S(2)}) async-start(), calls=%async_computation.1 | async-start | bytes 294912 | tf_op jit(solution)/shard_map/reduce_scatter | solution.py:88
  (53 other events, 783.4 us)
Sparse Core Ops, SparseCore 0:
  275.1 261.5 all-gather.2
  539.5 75.6 reduce-scatter.1
where the time goes:
time: 627 us; the launch traced here: 623 us
  waiting for transfers between devices  384 us (61%)
  starting transfers between devices  180 us (29%)
  matrix products  19.1 us (3%)
  local copies, waits for them, and re-layouts  17.3 us (3%)
  between operations  14.1 us (2%)
  other arithmetic  7.64 us (1%)
    all_gather x1, waiting for transfers between devices, body(): lax.all_gather(flat_rows, ('ctx', 'rep'), axis=0, tiled=True)  262 us
    ppermute x64, starting transfers between devices, passed_along(): return lax.ppermute(value, axis, pairs)  180 us
    reduce_scatter x1, waiting for transfers between devices, body(): lax.psum_scatter(terms, 'kvh', scatter_dimension=0, tiled=True)  75.9 us
    ppermute x64, waiting for transfers between devices, passed_along(): return lax.ppermute(value, axis, pairs)  46.8 us
    while x32, local copies, waits for them, and re-layouts  14.2 us
  transfers between devices with their start and end apart: 66, of which 31 were waited for; matrix products, arithmetic and copies ran while one was open for 0% of the time, Pallas kernels for 0%

commit v1 on v0

v1 whole, which is shorter than its diff:
```python
import math

import jax
import jax.numpy as jnp
from jax import lax
from jax.sharding import PartitionSpec as P

FAR_BELOW = -1e30


def split_two(value):
    high = lax.reduce_precision(value, 8, 7)
    return high.astype(jnp.bfloat16), (value - high).astype(jnp.bfloat16)


def join_two(high, low):
    return high.astype(jnp.float32) + low.astype(jnp.float32)


def gathered(block, axes):
    count = lax.axis_size(axes)
    copies = jnp.broadcast_to(block[None], (count,) + block.shape)
    return lax.all_to_all(copies, axes, 0, 0, tiled=False)


def suffix_state(queries, suffix_keys, suffix_values, suffix_len, factor):
    cont_local, heads_local, head_dim = queries.shape
    key_set = suffix_keys[:, :, 0, :]
    value_set = suffix_values[:, :, 0, :]
    scores = (
        jnp.einsum("cqd,cud->cqu", queries, key_set, preferred_element_type=jnp.float32) * factor
    )
    live = lax.broadcasted_iota(jnp.int32, scores.shape, 2) < suffix_len[:, None, None]
    scores = jnp.where(live, scores, FAR_BELOW)
    highest = jnp.max(scores, axis=2)
    weights = jnp.where(live, jnp.exp(scores - highest[:, :, None]), 0.0)
    totals = jnp.sum(weights, axis=2)
    numer = jnp.einsum(
        "cqu,cud->cqd", weights.astype(jnp.bfloat16), value_set, preferred_element_type=jnp.float32
    )
    rows = cont_local * heads_local
    return (numer.reshape(rows, head_dim), highest.reshape(rows), totals.reshape(rows))


def body(queries, prompt_keys, prompt_values, suffix_keys, suffix_values, suffix_len, out_weight):
    cont_local, heads_local, head_dim = queries.shape
    factor = 1.0 / math.sqrt(head_dim)
    rows = cont_local * heads_local
    ctx = lax.axis_size("ctx")
    key_block = prompt_keys[:, 0, :]
    value_block = prompt_values[:, 0, :]
    home_numer, home_highest, home_totals = suffix_state(
        queries, suffix_keys, suffix_values, suffix_len, factor
    )

    with jax.named_scope("gather_queries"):
        visiting = gathered(queries.reshape(rows, head_dim), "ctx").reshape(ctx * rows, head_dim)
    with jax.named_scope("prompt_attention"):
        scores = (
            lax.dot_general(
                visiting, key_block, (((1,), (1,)), ((), ())), preferred_element_type=jnp.float32
            )
            * factor
        )
        highest = jnp.max(scores, axis=1)
        weights = jnp.exp(scores - highest[:, None])
        totals = jnp.sum(weights, axis=1)
        numer = jnp.dot(
            weights.astype(jnp.bfloat16), value_block, preferred_element_type=jnp.float32
        )
    with jax.named_scope("return_partials"):
        stats = jnp.stack(split_two(highest) + split_two(totals))
        stats = stats.reshape(4, ctx, rows).transpose(1, 0, 2).reshape(ctx, 4 * rows // head_dim, head_dim)
        sent = jnp.concatenate([numer.astype(jnp.bfloat16).reshape(ctx, rows, head_dim), stats], axis=1)
        back = lax.all_to_all(sent, "ctx", 0, 0, tiled=False)
    with jax.named_scope("combine"):
        numers = back[:, :rows].astype(jnp.float32)
        stats = back[:, rows:].reshape(ctx, 4, rows)
        highs = join_two(stats[:, 0], stats[:, 1])
        sums = join_two(stats[:, 2], stats[:, 3])
        joint = jnp.maximum(jnp.max(highs, axis=0), home_highest)
        scale = jnp.exp(highs - joint)
        home_scale = jnp.exp(home_highest - joint)
        total = jnp.sum(scale * sums, axis=0) + home_scale * home_totals
        numer = jnp.sum(scale[:, :, None] * numers, axis=0) + home_scale[:, None] * home_numer
        attended = (numer / total[:, None]).astype(jnp.bfloat16)
    attended_heads = attended.reshape(cont_local, heads_local, head_dim)
    with jax.named_scope("gather_attended"):
        flat_rows = attended.reshape(cont_local, heads_local * head_dim)
        everyone = gathered(flat_rows, ("ctx", "rep"))
        everyone = everyone.reshape(-1, heads_local * head_dim)
    with jax.named_scope("project"):
        terms = jnp.dot(everyone, out_weight, preferred_element_type=jnp.float32)
        terms = terms.astype(jnp.bfloat16)
    with jax.named_scope("sum_heads"):
        kvh = lax.axis_size("kvh")
        terms = terms.reshape(kvh, terms.shape[0] // kvh, terms.shape[1])
        parts = lax.all_to_all(terms, "kvh", 0, 0, tiled=False)
        projected = jnp.sum(parts.astype(jnp.float32), axis=0).astype(jnp.bfloat16)
    return (attended_heads, projected)


def solution(mesh):
    in_specs = (
        P(("ctx", "rep"), "kvh", None),
        P("ctx", "kvh", None),
        P("ctx", "kvh", None),
        P(("ctx", "rep"), None, "kvh", None),
        P(("ctx", "rep"), None, "kvh", None),
        P(("ctx", "rep")),
        P("kvh", ("ctx", "rep")),
    )
    out_specs = (P(("ctx", "rep"), "kvh", None), P("kvh", ("ctx", "rep")))
    return jax.shard_map(body, mesh=mesh, in_specs=in_specs, out_specs=out_specs, check_vma=False)
```

time: 627 us -> 119 us (0.19)
  waiting for transfers between devices: 384 us -> 9.2 us
  starting transfers between devices: 180 us -> 3.54 us
  blocking collectives: 0 us -> 72.3 us
  local copies, waits for them, and re-layouts: 17.3 us -> 2.26 us
  between operations: 14.1 us -> 0.77 us
    all_gather x1 -> x0, waiting for transfers between devices: 262 us -> none  [body(): lax.all_gather(flat_rows, ('ctx', 'rep'), axis=0, tiled=True)]
    ppermute x64 -> x0, starting transfers between devices: 180 us -> none  [passed_along(): return lax.ppermute(value, axis, pairs)]
    reduce_scatter x1 -> x0, waiting for transfers between devices: 75.9 us -> none  [body(): lax.psum_scatter(terms, 'kvh', scatter_dimension=0, tiled=True)]
    all_to_all x0 -> x3, blocking collectives: none -> 72.3 us  [the longest x2 56.3 us: gathered(): return lax.all_to_all(copies, axes, 0, 0, tiled=False)]
    ppermute x64 -> x0, waiting for transfers between devices: 46.8 us -> none  [passed_along(): return lax.ppermute(value, axis, pairs)]
    while x32 -> x0, local copies, waits for them, and re-layouts: 14.2 us -> none
    all_to_all x0 -> x1, waiting for transfers between devices: none -> 9.2 us  [body(): back = lax.all_to_all(sent, 'ctx', 0, 0, tiled=False)]
    dot_general x33 -> x3, matrix products: 16.4 us -> 18.4 us  [the longest x1 8.66 us: body(): jnp.dot(weights.astype(jnp.bfloat16), value_block, preferred_element_type...]
  transfers between devices with their start and end apart: 66 -> 1, of which waited for: 31 -> 1; matrix products, arithmetic and copies ran while one was open for 0% -> 1% of each run, Pallas kernels for 0% -> 0%
where the time goes in v1:
time: 119 us; the launch traced here: 118 us
  blocking collectives  72.3 us (61%)
  matrix products  19 us (16%)
  other arithmetic  11.2 us (9%)
  waiting for transfers between devices  9.2 us (8%)
  starting transfers between devices  3.54 us (3%)
  local copies, waits for them, and re-layouts  2.26 us (2%)
    all_to_all x2, blocking collectives, gathered(): return lax.all_to_all(copies, axes, 0, 0, tiled=False)  56.3 us
    all_to_all x1, blocking collectives, body(): parts = lax.all_to_all(terms, 'kvh', 0, 0, tiled=False)  16.1 us
    all_to_all x1, waiting for transfers between devices, body(): back = lax.all_to_all(sent, 'ctx', 0, 0, tiled=False)  9.2 us
    reduce_sum x1, other arithmetic, body(): totals = jnp.sum(weights, axis=1)  8.68 us
    dot_general x1, matrix products, body(): jnp.dot(weights.astype(jnp.bfloat16), value_block, preferred_element_type...  8.66 us
    dot_general x1, matrix products, body(): lax.dot_general(visiting, key_block, (((1,), (1,)), ((), ())), preferred_...  8.07 us
    all_to_all x1, starting transfers between devices, body(): back = lax.all_to_all(sent, 'ctx', 0, 0, tiled=False)  3.54 us
  transfers between devices with their start and end apart: 1, of which 1 were waited for; matrix products, arithmetic and copies ran while one was open for 1% of the time, Pallas kernels for 0%

profile of v1, /device:TPU:1, one launch (start us, length us, event | category | flops | bytes accessed | tf_op | source)
XLA Modules:
  0.0 118.3 jit_solution(18115324325534403461)
XLA Ops:
  0.6 0.0 copy-start
  0.6 0.8 broadcast_in_dim.14
  1.5 19.9 %all_to_all.20 = bf16[16,64,128]{2,1,0:T(8,128)(2,1)S(1)} all-to-all(bf16[16,64,128]{2,1,0:T(8,128)(2,1)S(1)} %broadcast_in_dim.14), channel_id=1, replica_groups=mesh['ctx'=16,'kvh'=8,'rep'=4] {'ctx'}, dimensions={0} | all-to-all | bytes 524288 | tf_op jit(solution)/shard_map/gather_queries/all_to_all | solution.py:23
  21.4 0.0 copy-done
  21.4 8.1 %multiply_reduce_fusion = (f32[1024]{0:T(1024)S(1)}, f32[1024,4096]{1,0:T(8,128)}) fusion(bf16[1024,128]{1,0:T(8,128)(2,1)S(1)} %bitcast.49, bf16[4096,1,128]{2,0,1:T(8,128)(2,1)S(1)} %copy-done), kind=kOutput, calls=%fused_computation.1 | convolution fusion | flops 1082129408 | bytes 18092032 | tf_op jit(solution)/shard_map/prompt_attention/dot_general | solution.py:60
  29.4 0.1 reduce_max.32
  29.5 8.7 %fusion = f32[1024]{0:T(1024)S(1)} fusion(f32[1024,4096]{1,0:T(8,128)} %get-tuple-element.17, f32[1024]{0:T(1024)S(1)} %get-tuple-element.16), kind=kLoop, calls=%fused_computation.2 | loop fusion | flops 12581888 | bytes 16785408 | tf_op jit(solution)/shard_map/prompt_attention/reduce_sum | solution.py:67
  38.2 0.0 copy-start.1
  38.2 0.1 reduce_sum.57
  38.3 0.1 reshape.208
  38.4 8.7 %fusion.4 = bf16[1024,128]{1,0:T(8,128)(2,1)S(1)} fusion(f32[1024,4096]{1,0:T(8,128)} %get-tuple-element.17, f32[1024]{0:T(1024)S(1)} %get-tuple-element.16, bf16[4096,1,128]{2,0,1:T(8,128)(2,1)} %param.9), kind=kOutput, calls=%fused_computation.5 | convolution fusion | flops 1086455808 | bytes 18092032 | tf_op jit(solution)/shard_map/prompt_attention/dot_general | solution.py:68
  47.1 0.7 pad_maximum_fusion
  47.8 3.5 %all-to-all-start.1 = ((bf16[16,66,128]{2,1,0:T(8,128)(2,1)}), bf16[16,66,128]{2,1,0:T(8,128)(2,1)S(1)}, u32[]{:S(2)}, u32[]{:S(2)}) async-start(bf16[16,66,128]{2,1,0:T(8,128)(2,1)} %pad_maximum_fusion), calls=%async_computation.1 | async-start | bytes 589824 | tf_op jit(solution)/shard_map/return_partials/all_to_all | solution.py:75
  51.3 0.0 copy-done.2
  51.4 0.0 copy-done.3
  51.4 0.0 copy-done.4
  51.4 0.3 fusion.31
  51.7 0.1 reshape.210
  51.8 0.2 fusion.13
  52.0 9.2 %all-to-all-done.1 = bf16[16,66,128]{2,1,0:T(8,128)(2,1)S(1)} async-done(((bf16[16,66,128]{2,1,0:T(8,128)(2,1)}), bf16[16,66,128]{2,1,0:T(8,128)(2,1)S(1)}, u32[]{:S(2)}, u32[]{:S(2)}) %all-to-all-start.1) | async-done | bytes 270368 | tf_op jit(solution)/shard_map/return_partials/all_to_all | solution.py:75
  61.2 0.1 reshape.209
  61.3 0.1 reduce_max.35
  61.4 0.1 reduce_sum.61
  61.5 0.2 multiply_reduce_fusion.1
  61.8 0.2 convolution_multiply_fusion.1
  62.0 0.7 broadcast_bitcast_fusion
  62.8 0.5 broadcast_in_dim.30
  63.3 36.4 %all_to_all.21 = bf16[64,4,2048]{2,1,0:T(4,128)(2,1)S(1)} all-to-all(bf16[64,4,2048]{2,1,0:T(4,128)(2,1)S(1)} %broadcast_in_dim.30), channel_id=1, replica_groups=mesh['ctx'=16,'kvh'=8,'rep'=4] {'ctx','rep'}, dimensions={0} | all-to-all | bytes 2097152 | tf_op jit(solution)/shard_map/gather_attended/all_to_all | solution.py:23
  99.7 0.3 reshape.211
  99.9 1.7 %convolution_convert_fusion = bf16[256,256]{1,0:T(8,128)(2,1)S(1)} fusion(bf16[256,2048]{1,0:T(8,128)(2,1)S(1)} %reshape.211, bf16[2048,256]{1,0:T(8,128)(2,1)} %param.13), kind=kOutput, calls=%fused_computation.6 | convolution fusion | flops 268500992 | bytes 2228224 | tf_op jit(solution)/shard_map/project/dot_general | solution.py:93
  101.6 16.1 %all_to_all.22 = bf16[8,32,256]{2,1,0:T(8,128)(2,1)S(1)} all-to-all(bf16[8,32,256]{2,1,0:T(8,128)(2,1)S(1)} %bitcast.50), channel_id=1, replica_groups=mesh['ctx'=16,'kvh'=8,'rep'=4] {'kvh'}, dimensions={0} | all-to-all | bytes 262144 | tf_op jit(solution)/shard_map/sum_heads/all_to_all | solution.py:98
  117.7 0.6 reduce_sum.64
  (15 shorter events, 0.2 us)
Async XLA Ops:
  0.6 20.7 %copy-start = (bf16[4096,1,128]{2,0,1:T(8,128)(2,1)S(1)}, bf16[4096,1,128]{2,0,1:T(8,128)(2,1)}, u32[]{:S(2)}) copy-start(bf16[4096,1,128]{2,0,1:T(8,128)(2,1)} %param.8) | copy-start | bytes 3145732
  29.5 21.8 %copy-start.2 = (bf16[4,512,1,128]{3,1,2,0:T(8,128)(2,1)S(1)}, bf16[4,512,1,128]{3,1,2,0:T(8,128)(2,1)}, u32[]{:S(2)}) copy-start(bf16[4,512,1,128]{3,1,2,0:T(8,128)(2,1)} %param.10) | copy-start | bytes 1572868
  29.5 21.8 %copy-start.3 = (bf16[4,16,128]{2,1,0:T(8,128)(2,1)S(1)}, bf16[4,16,128]{2,1,0:T(8,128)(2,1)}, u32[]{:S(2)}) copy-start(bf16[4,16,128]{2,1,0:T(8,128)(2,1)} %param.7) | copy-start | bytes 49156
  29.5 21.9 %copy-start.4 = (s32[4]{0:T(128)S(1)}, s32[4]{0:T(128)}, u32[]{:S(2)}) copy-start(s32[4]{0:T(128)} %param.12) | copy-start | bytes 52
  38.2 23.6 %copy-start.1 = (bf16[4,512,1,128]{3,1,2,0:T(8,128)(2,1)S(1)}, bf16[4,512,1,128]{3,1,2,0:T(8,128)(2,1)}, u32[]{:S(2)}) copy-start(bf16[4,512,1,128]{3,1,2,0:T(8,128)(2,1)} %param.11) | copy-start | bytes 1572868
  47.8 13.4 %all-to-all-start.1 = ((bf16[16,66,128]{2,1,0:T(8,128)(2,1)}), bf16[16,66,128]{2,1,0:T(8,128)(2,1)S(1)}, u32[]{:S(2)}, u32[]{:S(2)}) async-start(bf16[16,66,128]{2,1,0:T(8,128)(2,1)} %pad_maximum_fusion), calls=%async_computation.1 | async-start | bytes 589824 | tf_op jit(solution)/shard_map/return_partials/all_to_all | solution.py:75

commit v2 on v1

v2 whole, which is shorter than its diff:
```python
import functools
import math

import jax
import jax.numpy as jnp
from jax import lax
from jax.experimental import pallas as pl
from jax.experimental.pallas import tpu as pltpu
from jax.sharding import Mesh
from jax.sharding import PartitionSpec as P

FAR_BELOW = -1e30
CTX = ("y", "zl")
KVH = ("x", "core")
REP = ("zh",)
VMEM = pl.BlockSpec(memory_space=pltpu.VMEM)
SMEM = pl.BlockSpec(memory_space=pltpu.SMEM)
LAST_WITH_LAST = (((1,), (1,)), ((), ()))
FIRST_WITH_FIRST = (((0,), (0,)), ((), ()))
STAT_ROWS = 16


def base_two(head_dim):
    return math.log2(math.e) / math.sqrt(head_dim)


def gathered(copies, axes):
    return lax.all_to_all(copies, axes, 0, 0, tiled=False)


def suffix_kernel(len_ref, query_ref, key_ref, value_ref, numer_ref, stat_ref, *, conts):
    rows, head_dim = query_ref.shape
    slots = key_ref.shape[0] // conts
    twice = jnp.concatenate([query_ref[...]] * 2, axis=0)
    scores = lax.dot_general(
        key_ref[...], twice, LAST_WITH_LAST, preferred_element_type=jnp.float32
    )
    scores = scores.reshape(conts, slots, 2 * rows)
    lane = lax.broadcasted_iota(jnp.int32, (1, 2 * rows), 1) % rows
    place = lax.broadcasted_iota(jnp.int32, (slots, 2 * rows), 0)
    per_cont = rows // conts
    masked = []
    for c in range(conts):
        limit = jnp.where(lane // per_cont == c, len_ref[c], 0)
        masked.append(jnp.where(place < limit, scores[c], FAR_BELOW))
    scores = jnp.concatenate(masked, axis=0)
    highest = jnp.max(scores, axis=0, keepdims=True)
    weights = jnp.where(
        scores > 0.5 * FAR_BELOW, jnp.exp2((scores - highest) * base_two(head_dim)), 0.0
    )
    totals = jnp.sum(weights, axis=0, keepdims=True)
    numer = lax.dot_general(
        value_ref[...],
        weights.astype(jnp.bfloat16),
        FIRST_WITH_FIRST,
        preferred_element_type=jnp.float32,
    )
    numer_ref[...] = numer.T[:rows]
    stat_ref[...] = jnp.concatenate(
        [highest, totals, jnp.zeros((6, 2 * rows), jnp.float32)], axis=0
    )


def prompt_kernel(query_ref, key_ref, value_ref, out_ref):
    blocks, block_rows, head_dim = query_ref.shape
    rows = blocks * block_rows
    queries = query_ref[...].reshape(rows, head_dim)
    scores = lax.dot_general(
        key_ref[...], queries, LAST_WITH_LAST, preferred_element_type=jnp.float32
    )
    shift = jnp.max(scores, axis=0, keepdims=True).astype(jnp.bfloat16)
    weights = jnp.exp2((scores - shift.astype(jnp.float32)) * base_two(head_dim))
    totals = jnp.sum(weights, axis=0, keepdims=True)
    numer = lax.dot_general(
        value_ref[...],
        weights.astype(jnp.bfloat16),
        FIRST_WITH_FIRST,
        preferred_element_type=jnp.float32,
    )
    out_ref[:, :block_rows, :] = (
        numer.T.astype(jnp.bfloat16).reshape(blocks, block_rows, head_dim)
    )
    high = totals.astype(jnp.bfloat16)
    low = totals - high.astype(jnp.float32)
    stats = jnp.concatenate(
        [
            shift.astype(jnp.float32),
            high.astype(jnp.float32),
            low,
            jnp.zeros((STAT_ROWS - 3, rows), jnp.float32),
        ],
        axis=0,
    ).astype(jnp.bfloat16)
    for block in range(blocks):
        tile = block * block_rows // head_dim
        out_ref[block, block_rows:, :] = stats[:, tile * head_dim : (tile + 1) * head_dim]


def combine_kernel(half_ref, back_ref, numer_ref, stat_ref, out_ref, spread_ref):
    blocks, _, head_dim = back_ref.shape
    rows = out_ref.shape[0]
    stats = back_ref[:, rows:, :].astype(jnp.float32)
    highs = stats[:, 0, :]
    sums = stats[:, 1, :] + stats[:, 2, :]
    home_high = stat_ref[0:1, :]
    home_sum = stat_ref[1:2, :]
    joint = jnp.maximum(jnp.max(highs, axis=0, keepdims=True), home_high)
    scale = jnp.exp2((highs - joint) * base_two(head_dim))
    home_scale = jnp.exp2((home_high - joint) * base_two(head_dim))
    total = jnp.sum(scale * sums, axis=0, keepdims=True) + home_scale * home_sum
    factors = jnp.concatenate(
        [
            scale / total,
            home_scale / total,
            jnp.zeros((head_dim - blocks - 1, head_dim), jnp.float32),
        ],
        axis=0,
    )
    spread_ref[...] = factors.T
    factors = spread_ref[pl.ds(pl.multiple_of(half_ref[0] * rows, rows), rows), :]
    numer = numer_ref[...] * factors[:, blocks : blocks + 1]
    for block in range(blocks):
        numer += back_ref[block, :rows, :].astype(jnp.float32) * factors[:, block : block + 1]
    out_ref[...] = numer.astype(jnp.bfloat16)


def body(queries, prompt_keys, prompt_values, suffix_keys, suffix_values, suffix_len, out_weight):
    conts, heads, head_dim = queries.shape
    rows = conts * heads
    ctx = lax.axis_size(CTX)
    rep = lax.axis_size(REP)
    kvh = lax.axis_size(KVH)
    half = lax.axis_index("zl")
    tokens = prompt_keys.shape[0]
    slots = suffix_keys.shape[1]
    depth, width = out_weight.shape
    params = pltpu.CompilerParams(vmem_limit_bytes=48 * 2**20)
    query_rows = queries.reshape(rows, head_dim)

    with jax.named_scope("gather_queries"):
        visiting = gathered(
            jnp.broadcast_to(query_rows[None], (ctx, rows, head_dim)), CTX
        )
    with jax.named_scope("swap_weight"):
        halves = out_weight.reshape(2, depth // 2, width)
        kept = lax.dynamic_index_in_dim(halves, half, 0, keepdims=False)
        given = lax.dynamic_index_in_dim(halves, 1 - half, 0, keepdims=False)
        taken = lax.ppermute(given, "zl", [(0, 1), (1, 0)])
    with jax.named_scope("suffix_attention"):
        home_numer, home_stat = pl.pallas_call(
            functools.partial(suffix_kernel, conts=conts),
            in_specs=[SMEM, VMEM, VMEM, VMEM],
            out_specs=[VMEM, VMEM],
            out_shape=[
                jax.ShapeDtypeStruct((rows, head_dim), jnp.float32),
                jax.ShapeDtypeStruct((8, head_dim), jnp.float32),
            ],
            compiler_params=params,
            cost_estimate=pl.CostEstimate(
                flops=4 * conts * slots * head_dim * head_dim,
                bytes_accessed=4 * conts * slots * head_dim,
                transcendentals=conts * slots * head_dim,
            ),
        )(
            suffix_len,
            query_rows,
            suffix_keys.reshape(conts * slots, head_dim),
            suffix_values.reshape(conts * slots, head_dim),
        )
    with jax.named_scope("prompt_attention"):
        sent = pl.pallas_call(
            prompt_kernel,
            in_specs=[VMEM] * 3,
            out_specs=VMEM,
            out_shape=jax.ShapeDtypeStruct((ctx, rows + STAT_ROWS, head_dim), jnp.bfloat16),
            compiler_params=params,
            cost_estimate=pl.CostEstimate(
                flops=4 * ctx * rows * tokens * head_dim,
                bytes_accessed=4 * tokens * head_dim,
                transcendentals=ctx * rows * tokens,
            ),
        )(
            visiting,
            prompt_keys.reshape(tokens, head_dim),
            prompt_values.reshape(tokens, head_dim),
        )
    with jax.named_scope("return_partials"):
        back = lax.all_to_all(sent, CTX, 0, 0, tiled=False)
    with jax.named_scope("combine"):
        attended = pl.pallas_call(
            combine_kernel,
            in_specs=[SMEM, VMEM, VMEM, VMEM],
            out_specs=VMEM,
            out_shape=jax.ShapeDtypeStruct((rows, head_dim), jnp.bfloat16),
            scratch_shapes=[pltpu.VMEM((head_dim, head_dim), jnp.float32)],
            compiler_params=params,
        )(half.reshape(1), back, home_numer, home_stat)
    with jax.named_scope("gather_attended"):
        flat = attended.reshape(conts, 2, depth // 2).transpose(1, 0, 2)
        copies = jnp.broadcast_to(
            flat[None, :, None], (ctx // 2, 2, rep, conts, depth // 2)
        ).reshape(ctx * rep, conts, depth // 2)
        everyone = gathered(copies, CTX + REP).reshape(ctx * rep * conts, depth // 2)
    with jax.named_scope("project"):
        own = jnp.dot(everyone, kept, preferred_element_type=jnp.float32)
        other = jnp.dot(everyone, taken, preferred_element_type=jnp.float32)
        own, other = own.astype(jnp.bfloat16), other.astype(jnp.bfloat16)
    with jax.named_scope("sum_heads"):
        low = jnp.where(half == 0, own, other).reshape(kvh, -1, width)
        high = jnp.where(half == 0, other, own).reshape(kvh, -1, width)
        terms = jnp.stack([low, high], axis=1).reshape(2 * kvh, -1, width)
        parts = lax.all_to_all(terms, KVH + ("zl",), 0, 0, tiled=False)
        projected = jnp.sum(parts.astype(jnp.float32), axis=0).astype(jnp.bfloat16)
    return (attended.reshape(conts, heads, head_dim), projected)


def solution(mesh):
    ctx, kvh, rep = (mesh.shape[name] for name in ("ctx", "kvh", "rep"))
    fine = Mesh(
        mesh.devices.reshape(ctx // 2, 2, kvh // 2, 2, rep), ("y", "zl", "x", "core", "zh")
    )
    groups = CTX + REP
    in_specs = (
        P(groups, KVH, None),
        P(CTX, KVH, None),
        P(CTX, KVH, None),
        P(groups, None, KVH, None),
        P(groups, None, KVH, None),
        P(groups),
        P(KVH, groups),
    )
    out_specs = (P(groups, KVH, None), P(KVH, groups))
    return jax.shard_map(body, mesh=fine, in_specs=in_specs, out_specs=out_specs, check_vma=False)
```

time: 119 us -> 99.2 us (0.83)
  blocking collectives: 72.3 us -> 32.4 us
  waiting for transfers between devices: 9.2 us -> 30 us
  matrix products: 19 us -> 0.61 us
  starting transfers between devices: 3.54 us -> 18.8 us
  other arithmetic: 11.2 us -> 0.68 us
  Pallas kernels: 0 us -> 9.51 us
  local copies, waits for them, and re-layouts: 2.26 us -> 5.81 us
    all_to_all x2 -> x1, blocking collectives: 56.3 us -> 19.9 us  [gathered(): return lax.all_to_all(copies, axes, 0, 0, tiled=False)]
    dot_general x5 -> x2, matrix products: 19 us -> 0.61 us  [the longest x1 0.31 us: body(): own = jnp.dot(everyone, kept, preferred_element_type=jnp.float32)]
    all_to_all x1 -> x2, starting transfers between devices: 3.54 us -> 15.9 us  [the longest x1 12.2 us: gathered(): return lax.all_to_all(copies, axes, 0, 0, tiled=False)]
    all_to_all x1 -> x2, waiting for transfers between devices: 9.2 us -> 21.3 us  [the longest x1 13.4 us: gathered(): return lax.all_to_all(copies, axes, 0, 0, tiled=False)]
    pallas_call x0 -> x3, Pallas kernels: none -> 9.51 us  [the longest x1 6.88 us: body(): pl.pallas_call(prompt_kernel, in_specs=[VMEM] * 3, out_specs=VMEM, out_sh...]
    reduce_sum x4 -> x0, other arithmetic: 9.1 us -> none  [the longest x1 8.68 us: body(): totals = jnp.sum(weights, axis=1)]
    ppermute x0 -> x1, waiting for transfers between devices: none -> 8.7 us  [body(): taken = lax.ppermute(given, 'zl', [(0, 1), (1, 0)])]
    all_to_all x1, blocking collectives: 16.1 us -> 12.6 us  [body(): parts = lax.all_to_all(terms, KVH + ('zl',), 0, 0, tiled=False)]
  transfers between devices with their start and end apart: 1 -> 3, of which waited for: 1 -> 3; matrix products, arithmetic and copies ran while one was open for 1% -> 0% of each run, Pallas kernels for 0% -> 2%
where the time goes in v2:
time: 99.2 us; the launch traced here: 98.7 us
  blocking collectives  32.4 us (33%)
  waiting for transfers between devices  30 us (30%)
  starting transfers between devices  18.8 us (19%)
  Pallas kernels  9.51 us (10%)
  local copies, waits for them, and re-layouts  5.81 us (6%)
    all_to_all x1, blocking collectives, gathered(): return lax.all_to_all(copies, axes, 0, 0, tiled=False)  19.9 us
    all_to_all x1, waiting for transfers between devices, gathered(): return lax.all_to_all(copies, axes, 0, 0, tiled=False)  13.4 us
    all_to_all x1, blocking collectives, body(): parts = lax.all_to_all(terms, KVH + ('zl',), 0, 0, tiled=False)  12.6 us
    all_to_all x1, starting transfers between devices, gathered(): return lax.all_to_all(copies, axes, 0, 0, tiled=False)  12.2 us
    ppermute x1, waiting for transfers between devices, body(): taken = lax.ppermute(given, 'zl', [(0, 1), (1, 0)])  8.7 us
    all_to_all x1, waiting for transfers between devices, body(): back = lax.all_to_all(sent, CTX, 0, 0, tiled=False)  7.9 us
    pallas_call x1, Pallas kernels, body(): pl.pallas_call(prompt_kernel, in_specs=[VMEM] * 3, out_specs=VMEM, out_sh...  6.88 us
    all_to_all x1, starting transfers between devices, body(): back = lax.all_to_all(sent, CTX, 0, 0, tiled=False)  3.67 us
  transfers between devices with their start and end apart: 3, of which 3 were waited for; matrix products, arithmetic and copies ran while one was open for 0% of the time, Pallas kernels for 2%

profile of v2, /device:TPU:1, one launch (start us, length us, event | category | flops | bytes accessed | tf_op | source)
XLA Modules:
  0.0 98.7 jit_solution(396143654912230473)
XLA Ops:
  0.6 0.0 copy-start
  0.6 0.8 broadcast_in_dim.14
  1.5 19.9 %all_to_all.20.query_ref = bf16[16,64,128]{2,1,0:T(8,128)(2,1)S(1)} all-to-all(bf16[16,64,128]{2,1,0:T(8,128)(2,1)S(1)} %broadcast_in_dim.14), channel_id=1, replica_groups=mesh['y'=8,'zl'=2,'x'=4,'core'=2,'zh'=4] {'y','zl'}, dimensions={0} | all-to-all | bytes 524288 | tf_op jit(solution)/shard_map/gather_queries/all_to_all | solution.py:28
  21.4 0.0 copy-start.5
  21.4 1.2 %copy-done.5 = bf16[4096,1,128]{2,0,1:T(8,128)(2,1)S(1)} copy-done((bf16[4096,1,128]{2,0,1:T(8,128)(2,1)S(1)}, bf16[4096,1,128]{2,0,1:T(8,128)(2,1)}, u32[]{:S(2)}) %copy-start.5) | copy-done | bytes 1048600
  22.6 0.0 copy-start.6
  22.6 1.2 %copy-done.6 = bf16[4096,1,128]{2,0,1:T(8,128)(2,1)S(1)} copy-done((bf16[4096,1,128]{2,0,1:T(8,128)(2,1)S(1)}, bf16[4096,1,128]{2,0,1:T(8,128)(2,1)}, u32[]{:S(2)}) %copy-start.6) | copy-done | bytes 1048600
  23.8 0.0 copy-start.2
  23.8 6.9 %prompt_attention.1 = bf16[16,80,128]{2,1,0:T(8,128)(2,1)} custom-call(bf16[16,64,128]{2,1,0:T(8,128)(2,1)S(1)} %all_to_all.20.query_ref, bf16[4096,128]{1,0:T(8,128)(2,1)S(1)} %bitcast.31, bf16[4096,128]{1,0:T(8,128)(2,1)S(1)} %bitcast.32), custom_call_target="tpu_custom_call" | custom-call | flops 2147483648 | bytes 2097152 | tf_op jit(solution)/shard_map/prompt_attention/pallas_call | solution.py:171
  30.7 0.0 copy-start.1
  30.7 0.0 copy-start.3
  30.7 3.7 %all-to-all-start.1 = ((bf16[16,80,128]{2,1,0:T(8,128)(2,1)}), bf16[16,80,128]{2,1,0:T(8,128)(2,1)S(1)}, u32[]{:S(2)}, u32[]{:S(2)}) async-start(bf16[16,80,128]{2,1,0:T(8,128)(2,1)} %prompt_attention.1), calls=%async_computation.1 | async-start | bytes 655360 | tf_op jit(solution)/shard_map/return_partials/all_to_all | solution.py:188
  34.4 0.0 copy-start.4
  34.4 0.0 copy-done.2
  34.4 0.0 copy-done.1
  34.4 0.0 copy-done.3
  34.4 0.6 copy-done.4
  35.0 1.6 %suffix_attention.1 = (f32[64,128]{1,0:T(8,128)S(1)}, f32[8,128]{1,0:T(8,128)S(1)}) custom-call(s32[4]{0:T(128)S(1)} %copy-done.4, bf16[64,128]{1,0:T(8,128)(2,1)S(1)} %bitcast.30, bf16[2048,128]{1,0:T(8,128)(2,1)S(1)} %bitcast.27, bf16[2048,128]{1,0:T(8,128)(2,1)S(1)} %bitcast.28), custom_call_target="tpu_custom_call" | custom-call | flops 134217728 | bytes 1048576 | tf_op jit(solution)/shard_map/suffix_attention/pallas_call | solution.py:150
  36.7 7.9 %all-to-all-done.1.back_ref = bf16[16,80,128]{2,1,0:T(8,128)(2,1)S(1)} async-done(((bf16[16,80,128]{2,1,0:T(8,128)(2,1)}), bf16[16,80,128]{2,1,0:T(8,128)(2,1)S(1)}, u32[]{:S(2)}, u32[]{:S(2)}) %all-to-all-start.1) | async-done | bytes 327712 | tf_op jit(solution)/shard_map/return_partials/all_to_all | solution.py:188
  44.6 1.0 %combine.1 = bf16[64,128]{1,0:T(8,128)(2,1)} custom-call(s32[1]{0:T(128)} %bitcast.half_ref, bf16[16,80,128]{2,1,0:T(8,128)(2,1)S(1)} %all-to-all-done.1.back_ref, f32[64,128]{1,0:T(8,128)S(1)} %get-tuple-element.4.numer_ref, f32[8,128]{1,0:T(8,128)S(1)} %get-tuple-element.5.stat_ref), custom_call_target="tpu_custom_call" | custom-call | tf_op jit(solution)/shard_map/combine/pallas_call | solution.py:190
  45.6 0.7 reshape.52
  46.3 1.0 broadcast_in_dim.15
  47.3 12.2 %all-to-all-start.2 = ((bf16[64,4,1024]{2,1,0:T(4,128)(2,1)}), bf16[64,4,1024]{2,1,0:T(4,128)(2,1)S(1)}, u32[]{:S(2)}, u32[]{:S(2)}) async-start(bf16[64,4,1024]{2,1,0:T(4,128)(2,1)} %bitcast.8), calls=%async_computation.2 | async-start | bytes 1048576 | tf_op jit(solution)/shard_map/gather_attended/all_to_all | solution.py:28
  59.5 0.0 copy-done
  59.6 2.9 %collective-permute-start = (bf16[1024,256]{1,0:T(8,128)(2,1)S(1)}, bf16[1024,256]{1,0:T(8,128)(2,1)S(1)}, u32[]{:S(2)}, u32[]{:S(2)}) collective-permute-start(bf16[1024,256]{1,0:T(8,128)(2,1)S(1)} %dynamic-slice_bitcast_fusion), channel_id=1, source_target_pairs={{0,32},{32,0},{1,33},{33,1},{2,34},{34,2},{3,35},{35,3},{4,36},{36... | collective-permute-start | bytes 1572872 | tf_op jit(solution)/shard_map/swap_weight/ppermute | solution.py:148
  62.5 13.4 %all-to-all-done.2 = bf16[64,4,1024]{2,1,0:T(4,128)(2,1)S(1)} async-done(((bf16[64,4,1024]{2,1,0:T(4,128)(2,1)}), bf16[64,4,1024]{2,1,0:T(4,128)(2,1)S(1)}, u32[]{:S(2)}, u32[]{:S(2)}) %all-to-all-start.2) | async-done | bytes 524320 | tf_op jit(solution)/shard_map/gather_attended/all_to_all | solution.py:28
  75.9 0.1 reshape.54
  76.1 0.3 convolution_convert_fusion.1
  76.4 8.7 %collective-permute-done = bf16[1024,256]{1,0:T(8,128)(2,1)S(1)} collective-permute-done((bf16[1024,256]{1,0:T(8,128)(2,1)S(1)}, bf16[1024,256]{1,0:T(8,128)(2,1)S(1)}, u32[]{:S(2)}, u32[]{:S(2)}) %collective-permute-start) | collective-permute-done | bytes 524320 | tf_op jit(solution)/shard_map/swap_weight/ppermute | solution.py:148
  85.1 0.3 broadcast_select_fusion.1
  85.4 12.6 %all_to_all.21 = bf16[16,32,256]{2,1,0:T(8,128)(2,1)S(1)} all-to-all(bf16[16,32,256]{2,1,0:T(8,128)(2,1)S(1)} %bitcast.33), channel_id=1, replica_groups=mesh['y'=8,'zl'=2,'x'=4,'core'=2,'zh'=4] {'x','core','zl'}, dimensions={0} | all-to-all | bytes 524288 | tf_op jit(solution)/shard_map/sum_heads/all_to_all | solution.py:212
  98.0 0.6 reduce_sum.12
  (3 shorter events, 0.1 us)
Async XLA Ops:
  0.6 58.9 %copy-start = (bf16[2048,256]{1,0:T(8,128)(2,1)S(1)}, bf16[2048,256]{1,0:T(8,128)(2,1)}, u32[]{:S(2)}) copy-start(bf16[2048,256]{1,0:T(8,128)(2,1)} %param.13) | copy-start | bytes 3145732
  21.4 1.2 %copy-start.5 = (bf16[4096,1,128]{2,0,1:T(8,128)(2,1)S(1)}, bf16[4096,1,128]{2,0,1:T(8,128)(2,1)}, u32[]{:S(2)}) copy-start(bf16[4096,1,128]{2,0,1:T(8,128)(2,1)} %param.8) | copy-start | bytes 3145732
  22.6 1.2 %copy-start.6 = (bf16[4096,1,128]{2,0,1:T(8,128)(2,1)S(1)}, bf16[4096,1,128]{2,0,1:T(8,128)(2,1)}, u32[]{:S(2)}) copy-start(bf16[4096,1,128]{2,0,1:T(8,128)(2,1)} %param.9) | copy-start | bytes 3145732
  23.8 10.6 %copy-start.2 = (bf16[4,512,1,128]{3,1,2,0:T(8,128)(2,1)S(1)}, bf16[4,512,1,128]{3,1,2,0:T(8,128)(2,1)}, u32[]{:S(2)}) copy-start(bf16[4,512,1,128]{3,1,2,0:T(8,128)(2,1)} %param.11) | copy-start | bytes 1572868
  30.7 3.7 %copy-start.1 = (bf16[4,512,1,128]{3,1,2,0:T(8,128)(2,1)S(1)}, bf16[4,512,1,128]{3,1,2,0:T(8,128)(2,1)}, u32[]{:S(2)}) copy-start(bf16[4,512,1,128]{3,1,2,0:T(8,128)(2,1)} %param.10) | copy-start | bytes 1572868
  30.7 3.7 %copy-start.3 = (bf16[4,16,128]{2,1,0:T(8,128)(2,1)S(1)}, bf16[4,16,128]{2,1,0:T(8,128)(2,1)}, u32[]{:S(2)}) copy-start(bf16[4,16,128]{2,1,0:T(8,128)(2,1)} %param.7) | copy-start | bytes 49156
  30.7 13.9 %all-to-all-start.1 = ((bf16[16,80,128]{2,1,0:T(8,128)(2,1)}), bf16[16,80,128]{2,1,0:T(8,128)(2,1)S(1)}, u32[]{:S(2)}, u32[]{:S(2)}) async-start(bf16[16,80,128]{2,1,0:T(8,128)(2,1)} %prompt_attention.1), calls=%async_computation.1 | async-start | bytes 655360 | tf_op jit(solution)/shard_map/return_partials/all_to_all | solution.py:188
  34.4 0.7 copy-start.4
  47.3 28.7 %all-to-all-start.2 = ((bf16[64,4,1024]{2,1,0:T(4,128)(2,1)}), bf16[64,4,1024]{2,1,0:T(4,128)(2,1)S(1)}, u32[]{:S(2)}, u32[]{:S(2)}) async-start(bf16[64,4,1024]{2,1,0:T(4,128)(2,1)} %bitcast.8), calls=%async_computation.2 | async-start | bytes 1048576 | tf_op jit(solution)/shard_map/gather_attended/all_to_all | solution.py:28
  59.6 25.5 %collective-permute-start = (bf16[1024,256]{1,0:T(8,128)(2,1)S(1)}, bf16[1024,256]{1,0:T(8,128)(2,1)S(1)}, u32[]{:S(2)}, u32[]{:S(2)}) collective-permute-start(bf16[1024,256]{1,0:T(8,128)(2,1)S(1)} %dynamic-slice_bitcast_fusion), channel_id=1, source_target_pairs={{0,32},{32,0},{1,33},{33,1},{2,34},{34,2},{3,35},{35,3},{4,36},{36... | collective-permute-start | bytes 1572872 | tf_op jit(solution)/shard_map/swap_weight/ppermute | solution.py:148

commit v3 on v2

--- a/solution.py
+++ b/solution.py
@@ -61,9 +61,11 @@
     )
 
 
-def prompt_kernel(query_ref, key_ref, value_ref, out_ref):
+def prompt_kernel(query_ref, key_ref, value_hbm, out_ref, value_ref, value_sem):
     blocks, block_rows, head_dim = query_ref.shape
     rows = blocks * block_rows
+    copy = pltpu.make_async_copy(value_hbm, value_ref, value_sem)
+    copy.start()
     queries = query_ref[...].reshape(rows, head_dim)
     scores = lax.dot_general(
         key_ref[...], queries, LAST_WITH_LAST, preferred_element_type=jnp.float32
@@ -71,6 +73,7 @@
     shift = jnp.max(scores, axis=0, keepdims=True).astype(jnp.bfloat16)
     weights = jnp.exp2((scores - shift.astype(jnp.float32)) * base_two(head_dim))
     totals = jnp.sum(weights, axis=0, keepdims=True)
+    copy.wait()
     numer = lax.dot_general(
         value_ref[...],
         weights.astype(jnp.bfloat16),
@@ -96,7 +99,7 @@
         out_ref[block, block_rows:, :] = stats[:, tile * head_dim : (tile + 1) * head_dim]
 
 
-def combine_kernel(half_ref, back_ref, numer_ref, stat_ref, out_ref, spread_ref):
+def combine_kernel(half_ref, back_ref, numer_ref, stat_ref, out_ref, copies_ref, spread_ref, *, rep):
     blocks, _, head_dim = back_ref.shape
     rows = out_ref.shape[0]
     stats = back_ref[:, rows:, :].astype(jnp.float32)
@@ -122,6 +125,36 @@
     for block in range(blocks):
         numer += back_ref[block, :rows, :].astype(jnp.float32) * factors[:, block : block + 1]
     out_ref[...] = numer.astype(jnp.bfloat16)
+    slabs = numer.reshape(-1, 2, 8, head_dim)
+    parts = [
+        slabs[:, part].reshape(rows // 2, head_dim).astype(jnp.bfloat16) for part in range(2)
+    ]
+    for place in range(copies_ref.shape[0]):
+        copies_ref[place] = parts[place // rep % 2]
+
+
+def project_kernel(half_ref, block_ref, weight_ref, taken_ref, out_ref, wide_ref):
+    places, block_rows, head_dim = block_ref.shape
+    wide_ref[...] = block_ref[...].reshape(places * block_rows, head_dim).astype(jnp.float32)
+    heads = weight_ref.shape[0] // (2 * head_dim)
+    conts = places * block_rows // heads
+    left = jnp.concatenate(
+        [
+            wide_ref[pl.ds(head, conts, stride=heads), :].astype(jnp.bfloat16)
+            for head in range(heads)
+        ],
+        axis=1,
+    )
+    half = half_ref[0]
+    depth = heads * head_dim
+    kept = weight_ref[pl.ds(pl.multiple_of(half * depth, depth), depth), :]
+    own = jnp.dot(left, kept, preferred_element_type=jnp.float32).astype(jnp.bfloat16)
+    other = jnp.dot(left, taken_ref[...], preferred_element_type=jnp.float32).astype(jnp.bfloat16)
+    out_rows = out_ref.shape[1]
+    for group in range(out_ref.shape[0] // 2):
+        rows = slice(group * out_rows, (group + 1) * out_rows)
+        out_ref[2 * group + half] = own[rows]
+        out_ref[2 * group + 1 - half] = other[rows]
 
 
 def body(queries, prompt_keys, prompt_values, suffix_keys, suffix_values, suffix_len, out_weight):
@@ -134,7 +167,8 @@
     tokens = prompt_keys.shape[0]
     slots = suffix_keys.shape[1]
     depth, width = out_weight.shape
-    params = pltpu.CompilerParams(vmem_limit_bytes=48 * 2**20)
+    large = pltpu.CompilerParams(vmem_limit_bytes=40 * 2**20)
+    small = pltpu.CompilerParams(vmem_limit_bytes=12 * 2**20)
     query_rows = queries.reshape(rows, head_dim)
 
     with jax.named_scope("gather_queries"):
@@ -143,7 +177,6 @@
         )
     with jax.named_scope("swap_weight"):
         halves = out_weight.reshape(2, depth // 2, width)
-        kept = lax.dynamic_index_in_dim(halves, half, 0, keepdims=False)
         given = lax.dynamic_index_in_dim(halves, 1 - half, 0, keepdims=False)
         taken = lax.ppermute(given, "zl", [(0, 1), (1, 0)])
     with jax.named_scope("suffix_attention"):
@@ -155,7 +188,7 @@
                 jax.ShapeDtypeStruct((rows, head_dim), jnp.float32),
                 jax.ShapeDtypeStruct((8, head_dim), jnp.float32),
             ],
-            compiler_params=params,
+            compiler_params=small,
             cost_estimate=pl.CostEstimate(
                 flops=4 * conts * slots * head_dim * head_dim,
                 bytes_accessed=4 * conts * slots * head_dim,
@@ -167,13 +200,20 @@
             suffix_keys.reshape(conts * slots, head_dim),
             suffix_values.reshape(conts * slots, head_dim),
         )
+    visiting, home_numer, home_stat, taken = lax.optimization_barrier(
+        (visiting, home_numer, home_stat, taken)
+    )
     with jax.named_scope("prompt_attention"):
         sent = pl.pallas_call(
             prompt_kernel,
-            in_specs=[VMEM] * 3,
+            in_specs=[VMEM, VMEM, pl.BlockSpec(memory_space=pltpu.HBM)],
             out_specs=VMEM,
+            scratch_shapes=[
+                pltpu.VMEM((tokens, head_dim), jnp.bfloat16),
+                pltpu.SemaphoreType.DMA,
+            ],
             out_shape=jax.ShapeDtypeStruct((ctx, rows + STAT_ROWS, head_dim), jnp.bfloat16),
-            compiler_params=params,
+            compiler_params=large,
             cost_estimate=pl.CostEstimate(
                 flops=4 * ctx * rows * tokens * head_dim,
                 bytes_accessed=4 * tokens * head_dim,
@@ -182,33 +222,38 @@
         )(
             visiting,
             prompt_keys.reshape(tokens, head_dim),
-            prompt_values.reshape(tokens, head_dim),
+            pltpu.with_memory_space_constraint(
+                prompt_values.reshape(tokens, head_dim), pltpu.HBM
+            ),
         )
     with jax.named_scope("return_partials"):
         back = lax.all_to_all(sent, CTX, 0, 0, tiled=False)
     with jax.named_scope("combine"):
-        attended = pl.pallas_call(
-            combine_kernel,
+        attended, copies = pl.pallas_call(
+            functools.partial(combine_kernel, rep=rep),
+            in_specs=[SMEM, VMEM, VMEM, VMEM],
+            out_specs=[VMEM, VMEM],
+            out_shape=[
+                jax.ShapeDtypeStruct((rows, head_dim), jnp.bfloat16),
+                jax.ShapeDtypeStruct((ctx * rep, rows // 2, head_dim), jnp.bfloat16),
+            ],
+            scratch_shapes=[pltpu.VMEM((head_dim, head_dim), jnp.float32)],
+            compiler_params=small,
+        )(half.reshape(1), back, home_numer, home_stat)
+    with jax.named_scope("gather_attended"):
+        everyone = lax.all_to_all(copies, CTX + REP, 0, 0, tiled=False)
+    with jax.named_scope("project"):
+        terms = pl.pallas_call(
+            project_kernel,
             in_specs=[SMEM, VMEM, VMEM, VMEM],
             out_specs=VMEM,
-            out_shape=jax.ShapeDtypeStruct((rows, head_dim), jnp.bfloat16),
-            scratch_shapes=[pltpu.VMEM((head_dim, head_dim), jnp.float32)],
-            compiler_params=params,
-        )(half.reshape(1), back, home_numer, home_stat)
-    with jax.named_scope("gather_attended"):
-        flat = attended.reshape(conts, 2, depth // 2).transpose(1, 0, 2)
-        copies = jnp.broadcast_to(
-            flat[None, :, None], (ctx // 2, 2, rep, conts, depth // 2)
-        ).reshape(ctx * rep, conts, depth // 2)
-        everyone = gathered(copies, CTX + REP).reshape(ctx * rep * conts, depth // 2)
-    with jax.named_scope("project"):
-        own = jnp.dot(everyone, kept, preferred_element_type=jnp.float32)
-        other = jnp.dot(everyone, taken, preferred_element_type=jnp.float32)
-        own, other = own.astype(jnp.bfloat16), other.astype(jnp.bfloat16)
+            out_shape=jax.ShapeDtypeStruct(
+                (2 * kvh, ctx * rep * conts // kvh, width), jnp.bfloat16
+            ),
+            scratch_shapes=[pltpu.VMEM((ctx * rep * rows // 2, head_dim), jnp.float32)],
+            compiler_params=small,
+        )(half.reshape(1), everyone, out_weight, taken)
     with jax.named_scope("sum_heads"):
-        low = jnp.where(half == 0, own, other).reshape(kvh, -1, width)
-        high = jnp.where(half == 0, other, own).reshape(kvh, -1, width)
-        terms = jnp.stack([low, high], axis=1).reshape(2 * kvh, -1, width)
         parts = lax.all_to_all(terms, KVH + ("zl",), 0, 0, tiled=False)
         projected = jnp.sum(parts.astype(jnp.float32), axis=0).astype(jnp.bfloat16)
     return (attended.reshape(conts, heads, head_dim), projected)

time: 99.2 us -> 93.3 us (0.941)
  blocking collectives: 32.4 us -> 59.6 us
  waiting for transfers between devices: 30 us -> 7.76 us
  starting transfers between devices: 18.8 us -> 11.9 us
  local copies, waits for them, and re-layouts: 5.81 us -> 2.53 us
    all_to_all x1 -> x2, blocking collectives: 19.9 us -> 43.2 us  [the longest x1 28.6 us: body(): everyone = lax.all_to_all(copies, CTX + REP, 0, 0, tiled=False)]
    ppermute x1, waiting for transfers between devices: 8.7 us -> 0.01 us  [body(): taken = lax.ppermute(given, 'zl', [(0, 1), (1, 0)])]
    all_to_all x1 -> x0, waiting for transfers between devices: 7.9 us -> none  [body(): back = lax.all_to_all(sent, CTX, 0, 0, tiled=False)]
    all_to_all x1, waiting for transfers between devices: 13.4 us -> 7.76 us  [gathered(): return lax.all_to_all(copies, axes, 0, 0, tiled=False)]
    all_to_all x1, starting transfers between devices: 12.2 us -> 6.93 us  [gathered(): return lax.all_to_all(copies, axes, 0, 0, tiled=False)]
    all_to_all x1, blocking collectives: 12.6 us -> 16.3 us  [body(): parts = lax.all_to_all(terms, KVH + ('zl',), 0, 0, tiled=False)]
    all_to_all x1 -> x0, starting transfers between devices: 3.67 us -> none  [body(): back = lax.all_to_all(sent, CTX, 0, 0, tiled=False)]
    unnamed x14 -> x12, local copies, waits for them, and re-layouts: 3.09 us -> 0.65 us
  transfers between devices with their start and end apart: 3 -> 2, of which waited for: 3 -> 1; matrix products, arithmetic and copies ran while one was open for 0% -> 1% of each run, Pallas kernels for 2% -> 2%
where the time goes in v3:
time: 93.3 us; the launch traced here: 92.9 us
  blocking collectives  59.6 us (64%)
  starting transfers between devices  11.9 us (13%)
  Pallas kernels  9.78 us (10%)
  waiting for transfers between devices  7.76 us (8%)
  local copies, waits for them, and re-layouts  2.53 us (3%)
    all_to_all x1, blocking collectives, body(): everyone = lax.all_to_all(copies, CTX + REP, 0, 0, tiled=False)  28.6 us
    all_to_all x1, blocking collectives, body(): parts = lax.all_to_all(terms, KVH + ('zl',), 0, 0, tiled=False)  16.3 us
    all_to_all x1, blocking collectives, body(): back = lax.all_to_all(sent, CTX, 0, 0, tiled=False)  14.7 us
    all_to_all x1, waiting for transfers between devices, gathered(): return lax.all_to_all(copies, axes, 0, 0, tiled=False)  7.76 us
    all_to_all x1, starting transfers between devices, gathered(): return lax.all_to_all(copies, axes, 0, 0, tiled=False)  6.93 us
    pallas_call x1, Pallas kernels, body(): pl.pallas_call(prompt_kernel, in_specs=[VMEM, VMEM, pl.BlockSpec(memory_s...  6.64 us
    ppermute x1, starting transfers between devices, body(): taken = lax.ppermute(given, 'zl', [(0, 1), (1, 0)])  4.96 us
  transfers between devices with their start and end apart: 2, of which 1 were waited for; matrix products, arithmetic and copies ran while one was open for 1% of the time, Pallas kernels for 2%

profile of v3, /device:TPU:1, one launch (start us, length us, event | category | flops | bytes accessed | tf_op | source)
XLA Modules:
  0.0 92.9 jit_solution(11641693931907349772)
XLA Ops:
  0.6 0.0 copy-start.3
  0.6 0.0 copy-start.2
  0.7 1.1 %dynamic-slice_bitcast_fusion = bf16[1024,256]{1,0:T(8,128)(2,1)S(1)} fusion(bf16[2,1024,256]{2,1,0:T(8,128)(2,1)} %bitcast.10, s32[]{:T(128)S(6)} %select_n.4), kind=kLoop, calls=%fused_computation | loop fusion | bytes 1048580 | tf_op jit(solution)/shard_map/swap_weight/jit(dynamic_index_in_dim)/squeeze | solution.py:180
  1.8 0.0 copy-start.1
  1.8 5.0 %collective-permute-start = (bf16[1024,256]{1,0:T(8,128)(2,1)S(1)}, bf16[1024,256]{1,0:T(8,128)(2,1)S(1)}, u32[]{:S(2)}, u32[]{:S(2)}) collective-permute-start(bf16[1024,256]{1,0:T(8,128)(2,1)S(1)} %dynamic-slice_bitcast_fusion), channel_id=1, source_target_pairs={{0,32},{32,0},{1,33},{33,1},{2,34},{34,2},{3,35},{35,3},{4,36},{36... | collective-permute-start | bytes 1572872 | tf_op jit(solution)/shard_map/swap_weight/ppermute | solution.py:181
  6.8 0.0 copy-done.3
  6.8 0.7 broadcast_in_dim.8
  7.5 6.9 %all-to-all-start = ((bf16[16,64,128]{2,1,0:T(8,128)(2,1)}), bf16[16,64,128]{2,1,0:T(8,128)(2,1)S(1)}, u32[]{:S(2)}, u32[]{:S(2)}) async-start(bf16[16,64,128]{2,1,0:T(8,128)(2,1)} %broadcast_in_dim.8), calls=%async_computation | async-start | bytes 524288 | tf_op jit(solution)/shard_map/gather_queries/all_to_all | solution.py:28
  14.5 0.0 copy-start.4
  14.5 0.0 copy-start.5
  14.5 0.0 copy-done.2
  14.5 0.0 copy-done.1
  14.5 0.6 copy-done.4
  15.1 1.6 %suffix_attention.1 = (f32[64,128]{1,0:T(8,128)S(1)}, f32[8,128]{1,0:T(8,128)S(1)}) custom-call(s32[4]{0:T(128)S(1)} %copy-done.4, bf16[64,128]{1,0:T(8,128)(2,1)S(1)} %bitcast.14, bf16[2048,128]{1,0:T(8,128)(2,1)S(1)} %bitcast.11, bf16[2048,128]{1,0:T(8,128)(2,1)S(1)} %bitcast.12), custom_call_target="tpu_custom_call" | custom-call | flops 134217728 | bytes 1048576 | tf_op jit(solution)/shard_map/suffix_attention/pallas_call | solution.py:183
  16.7 7.8 %all-to-all-done.query_ref = bf16[16,64,128]{2,1,0:T(8,128)(2,1)S(1)} async-done(((bf16[16,64,128]{2,1,0:T(8,128)(2,1)}), bf16[16,64,128]{2,1,0:T(8,128)(2,1)S(1)}, u32[]{:S(2)}, u32[]{:S(2)}) %all-to-all-start) | async-done | bytes 262176 | tf_op jit(solution)/shard_map/gather_queries/all_to_all | solution.py:28
  24.5 0.0 collective-permute-done.taken_ref
  24.5 0.0 copy-done.5
  24.5 6.6 %prompt_attention.1 = bf16[16,80,128]{2,1,0:T(8,128)(2,1)S(1)} custom-call(bf16[16,64,128]{2,1,0:T(8,128)(2,1)S(1)} %all-to-all-done.query_ref, bf16[4096,128]{1,0:T(8,128)(2,1)S(1)} %bitcast.15, bf16[4096,128]{1,0:T(8,128)(2,1)} %bitcast.16), custom_call_target="tpu_custom_call" | custom-call | flops 2147483648 | bytes 2097152 | tf_op jit(solution)/shard_map/prompt_attention/pallas_call | solution.py:207
  31.1 0.0 copy-start
  31.2 14.7 %all_to_all.20.back_ref = bf16[16,80,128]{2,1,0:T(8,128)(2,1)S(1)} all-to-all(bf16[16,80,128]{2,1,0:T(8,128)(2,1)S(1)} %prompt_attention.1), channel_id=1, replica_groups=mesh['y'=8,'zl'=2,'x'=4,'core'=2,'zh'=4] {'y','zl'}, dimensions={0} | all-to-all | bytes 655360 | tf_op jit(solution)/shard_map/return_partials/all_to_all | solution.py:230
  45.8 1.0 %combine.1 = (bf16[64,128]{1,0:T(8,128)(2,1)}, bf16[64,32,128]{2,1,0:T(8,128)(2,1)S(1)}) custom-call(s32[1]{0:T(128)} %bitcast.half_ref, bf16[16,80,128]{2,1,0:T(8,128)(2,1)S(1)} %all_to_all.20.back_ref, f32[64,128]{1,0:T(8,128)S(1)} %get-tuple-element.13.numer_ref, f32[8,128]{1,0:T(8,128)S(1)} %get-tuple-element.14.stat_ref), custom_call_target="tpu_custom_call" | custom-call | tf_op jit(solution)/shard_map/combine/pallas_call | solution.py:232
  46.9 28.6 %all_to_all.21.block_ref = bf16[64,32,128]{2,1,0:T(8,128)(2,1)S(1)} all-to-all(bf16[64,32,128]{2,1,0:T(8,128)(2,1)S(1)} %get-tuple-element.16), channel_id=1, replica_groups=mesh['y'=8,'zl'=2,'x'=4,'core'=2,'zh'=4] {'y','zl','zh'}, dimensions={0} | all-to-all | bytes 1048576 | tf_op jit(solution)/shard_map/gather_attended/all_to_all | solution.py:244
  75.4 0.0 copy-done
  75.4 0.5 project.1
  76.0 16.3 %all_to_all.22 = bf16[16,32,256]{2,1,0:T(8,128)(2,1)S(1)} all-to-all(bf16[16,32,256]{2,1,0:T(8,128)(2,1)S(1)} %project.1), channel_id=1, replica_groups=mesh['y'=8,'zl'=2,'x'=4,'core'=2,'zh'=4] {'x','core','zl'}, dimensions={0} | all-to-all | bytes 524288 | tf_op jit(solution)/shard_map/sum_heads/all_to_all | solution.py:257
  92.3 0.6 reduce_sum.12
Async XLA Ops:
  0.6 6.1 %copy-start.3 = (bf16[4,16,128]{2,1,0:T(8,128)(2,1)S(1)}, bf16[4,16,128]{2,1,0:T(8,128)(2,1)}, u32[]{:S(2)}) copy-start(bf16[4,16,128]{2,1,0:T(8,128)(2,1)} %param.7) | copy-start | bytes 49156
  0.6 13.8 %copy-start.2 = (bf16[4,512,1,128]{3,1,2,0:T(8,128)(2,1)S(1)}, bf16[4,512,1,128]{3,1,2,0:T(8,128)(2,1)}, u32[]{:S(2)}) copy-start(bf16[4,512,1,128]{3,1,2,0:T(8,128)(2,1)} %param.11) | copy-start | bytes 1572868
  1.8 12.7 %copy-start.1 = (bf16[4,512,1,128]{3,1,2,0:T(8,128)(2,1)S(1)}, bf16[4,512,1,128]{3,1,2,0:T(8,128)(2,1)}, u32[]{:S(2)}) copy-start(bf16[4,512,1,128]{3,1,2,0:T(8,128)(2,1)} %param.10) | copy-start | bytes 1572868
  1.8 22.7 %collective-permute-start = (bf16[1024,256]{1,0:T(8,128)(2,1)S(1)}, bf16[1024,256]{1,0:T(8,128)(2,1)S(1)}, u32[]{:S(2)}, u32[]{:S(2)}) collective-permute-start(bf16[1024,256]{1,0:T(8,128)(2,1)S(1)} %dynamic-slice_bitcast_fusion), channel_id=1, source_target_pairs={{0,32},{32,0},{1,33},{33,1},{2,34},{34,2},{3,35},{35,3},{4,36},{36... | collective-permute-start | bytes 1572872 | tf_op jit(solution)/shard_map/swap_weight/ppermute | solution.py:181
  7.5 17.0 %all-to-all-start = ((bf16[16,64,128]{2,1,0:T(8,128)(2,1)}), bf16[16,64,128]{2,1,0:T(8,128)(2,1)S(1)}, u32[]{:S(2)}, u32[]{:S(2)}) async-start(bf16[16,64,128]{2,1,0:T(8,128)(2,1)} %broadcast_in_dim.8), calls=%async_computation | async-start | bytes 524288 | tf_op jit(solution)/shard_map/gather_queries/all_to_all | solution.py:28
  14.5 0.7 copy-start.4
  14.5 10.0 %copy-start.5 = (bf16[4096,1,128]{2,0,1:T(8,128)(2,1)S(1)}, bf16[4096,1,128]{2,0,1:T(8,128)(2,1)}, u32[]{:S(2)}) copy-start(bf16[4096,1,128]{2,0,1:T(8,128)(2,1)} %param.8) | copy-start | bytes 3145732
  31.1 44.3 %copy-start = (bf16[2048,256]{1,0:T(8,128)(2,1)S(1)}, bf16[2048,256]{1,0:T(8,128)(2,1)}, u32[]{:S(2)}) copy-start(bf16[2048,256]{1,0:T(8,128)(2,1)} %weight_ref.1) | copy-start | bytes 3145732

commit v4 on v3

--- a/solution.py
+++ b/solution.py
@@ -17,7 +17,7 @@
 SMEM = pl.BlockSpec(memory_space=pltpu.SMEM)
 LAST_WITH_LAST = (((1,), (1,)), ((), ()))
 FIRST_WITH_FIRST = (((0,), (0,)), ((), ()))
-STAT_ROWS = 16
+STAT_ROWS = 8
 
 
 def base_two(head_dim):
@@ -133,7 +133,7 @@
         copies_ref[place] = parts[place // rep % 2]
 
 
-def project_kernel(half_ref, block_ref, weight_ref, taken_ref, out_ref, wide_ref):
+def project_kernel(half_ref, block_ref, weight_ref, upper_ref, lower_ref, out_ref, wide_ref):
     places, block_rows, head_dim = block_ref.shape
     wide_ref[...] = block_ref[...].reshape(places * block_rows, head_dim).astype(jnp.float32)
     heads = weight_ref.shape[0] // (2 * head_dim)
@@ -149,7 +149,10 @@
     depth = heads * head_dim
     kept = weight_ref[pl.ds(pl.multiple_of(half * depth, depth), depth), :]
     own = jnp.dot(left, kept, preferred_element_type=jnp.float32).astype(jnp.bfloat16)
-    other = jnp.dot(left, taken_ref[...], preferred_element_type=jnp.float32).astype(jnp.bfloat16)
+    cut = upper_ref.shape[0]
+    other = jnp.dot(left[:, :cut], upper_ref[...], preferred_element_type=jnp.float32)
+    other += jnp.dot(left[:, cut:], lower_ref[...], preferred_element_type=jnp.float32)
+    other = other.astype(jnp.bfloat16)
     out_rows = out_ref.shape[1]
     for group in range(out_ref.shape[0] // 2):
         rows = slice(group * out_rows, (group + 1) * out_rows)
@@ -178,7 +181,10 @@
     with jax.named_scope("swap_weight"):
         halves = out_weight.reshape(2, depth // 2, width)
         given = lax.dynamic_index_in_dim(halves, 1 - half, 0, keepdims=False)
-        taken = lax.ppermute(given, "zl", [(0, 1), (1, 0)])
+        cut = depth // 8 * 3
+        taken = [
+            lax.ppermute(part, "zl", [(0, 1), (1, 0)]) for part in (given[:cut], given[cut:])
+        ]
     with jax.named_scope("suffix_attention"):
         home_numer, home_stat = pl.pallas_call(
             functools.partial(suffix_kernel, conts=conts),
@@ -200,8 +206,8 @@
             suffix_keys.reshape(conts * slots, head_dim),
             suffix_values.reshape(conts * slots, head_dim),
         )
-    visiting, home_numer, home_stat, taken = lax.optimization_barrier(
-        (visiting, home_numer, home_stat, taken)
+    visiting, home_numer, home_stat = lax.optimization_barrier(
+        (visiting, home_numer, home_stat)
     )
     with jax.named_scope("prompt_attention"):
         sent = pl.pallas_call(
@@ -226,6 +232,7 @@
                 prompt_values.reshape(tokens, head_dim), pltpu.HBM
             ),
         )
+    sent, taken[0] = lax.optimization_barrier((sent, taken[0]))
     with jax.named_scope("return_partials"):
         back = lax.all_to_all(sent, CTX, 0, 0, tiled=False)
     with jax.named_scope("combine"):
@@ -240,19 +247,20 @@
             scratch_shapes=[pltpu.VMEM((head_dim, head_dim), jnp.float32)],
             compiler_params=small,
         )(half.reshape(1), back, home_numer, home_stat)
+    copies, taken[1] = lax.optimization_barrier((copies, taken[1]))
     with jax.named_scope("gather_attended"):
         everyone = lax.all_to_all(copies, CTX + REP, 0, 0, tiled=False)
     with jax.named_scope("project"):
         terms = pl.pallas_call(
             project_kernel,
-            in_specs=[SMEM, VMEM, VMEM, VMEM],
+            in_specs=[SMEM, VMEM, VMEM, VMEM, VMEM],
             out_specs=VMEM,
             out_shape=jax.ShapeDtypeStruct(
                 (2 * kvh, ctx * rep * conts // kvh, width), jnp.bfloat16
             ),
             scratch_shapes=[pltpu.VMEM((ctx * rep * rows // 2, head_dim), jnp.float32)],
             compiler_params=small,
-        )(half.reshape(1), everyone, out_weight, taken)
+        )(half.reshape(1), everyone, out_weight, taken[0], taken[1])
     with jax.named_scope("sum_heads"):
         parts = lax.all_to_all(terms, KVH + ("zl",), 0, 0, tiled=False)
         projected = jnp.sum(parts.astype(jnp.float32), axis=0).astype(jnp.bfloat16)

time: 93.3 us -> 91.9 us (0.985)
  blocking collectives: 59.6 us -> 45 us
  starting transfers between devices: 11.9 us -> 20.5 us
  waiting for transfers between devices: 7.76 us -> 10.8 us
    all_to_all x1 -> x0, blocking collectives: 14.7 us -> none  [body(): back = lax.all_to_all(sent, CTX, 0, 0, tiled=False)]
    all_to_all x0 -> x1, waiting for transfers between devices: none -> 6.92 us  [body(): back = lax.all_to_all(sent, CTX, 0, 0, tiled=False)]
    all_to_all x0 -> x1, starting transfers between devices: none -> 4.28 us  [body(): back = lax.all_to_all(sent, CTX, 0, 0, tiled=False)]
    all_to_all x1, waiting for transfers between devices: 7.76 us -> 3.84 us  [gathered(): return lax.all_to_all(copies, axes, 0, 0, tiled=False)]
    all_to_all x1, starting transfers between devices: 6.93 us -> 9.69 us  [gathered(): return lax.all_to_all(copies, axes, 0, 0, tiled=False)]
    ppermute x1 -> x2, starting transfers between devices: 4.96 us -> 6.54 us  [body(): lax.ppermute(part, 'zl', [(0, 1), (1, 0)])]
    squeeze x1 -> x0, local copies, waits for them, and re-layouts: 1.14 us -> none  [body(): given = lax.dynamic_index_in_dim(halves, 1 - half, 0, keepdims=False)]
    slice x0 -> x2, local copies, waits for them, and re-layouts: none -> 1.1 us  [the longest x1 1.08 us: body(): given[:cut]]
  transfers between devices with their start and end apart: 2 -> 4, of which waited for: 1 -> 2; matrix products, arithmetic and copies ran while one was open for 1% -> 1% of each run, Pallas kernels for 2% -> 11%
where the time goes in v4:
time: 91.9 us; the launch traced here: 91.4 us
  blocking collectives  45 us (49%)
  starting transfers between devices  20.5 us (22%)
  waiting for transfers between devices  10.8 us (12%)
  Pallas kernels  10.5 us (11%)
  local copies, waits for them, and re-layouts  3.21 us (3%)
    all_to_all x1, blocking collectives, body(): everyone = lax.all_to_all(copies, CTX + REP, 0, 0, tiled=False)  28.8 us
    all_to_all x1, blocking collectives, body(): parts = lax.all_to_all(terms, KVH + ('zl',), 0, 0, tiled=False)  16.1 us
    all_to_all x1, starting transfers between devices, gathered(): return lax.all_to_all(copies, axes, 0, 0, tiled=False)  9.69 us
    pallas_call x1, Pallas kernels, body(): pl.pallas_call(prompt_kernel, in_specs=[VMEM, VMEM, pl.BlockSpec(memory_s...  7.34 us
    all_to_all x1, waiting for transfers between devices, body(): back = lax.all_to_all(sent, CTX, 0, 0, tiled=False)  6.92 us
    ppermute x2, starting transfers between devices, body(): lax.ppermute(part, 'zl', [(0, 1), (1, 0)])  6.54 us
    all_to_all x1, starting transfers between devices, body(): back = lax.all_to_all(sent, CTX, 0, 0, tiled=False)  4.28 us
    all_to_all x1, waiting for transfers between devices, gathered(): return lax.all_to_all(copies, axes, 0, 0, tiled=False)  3.84 us
  transfers between devices with their start and end apart: 4, of which 2 were waited for; matrix products, arithmetic and copies ran while one was open for 1% of the time, Pallas kernels for 11%

profile of v4, /device:TPU:1, one launch (start us, length us, event | category | flops | bytes accessed | tf_op | source)
XLA Modules:
  0.0 91.4 jit_solution(7308347294199258552)
XLA Ops:
  0.6 1.5 %broadcast_in_dim.8 = bf16[16,64,128]{2,1,0:T(8,128)(2,1)} broadcast(bf16[64,128]{1,0:T(8,128)(2,1)} %bitcast.16), dimensions={1,2} | broadcast | bytes 278528 | tf_op jit(solution)/shard_map/gather_queries/broadcast_in_dim | solution.py:179
  2.1 0.0 copy-start.2
  2.1 9.7 %all-to-all-start = ((bf16[16,64,128]{2,1,0:T(8,128)(2,1)}), bf16[16,64,128]{2,1,0:T(8,128)(2,1)S(1)}, u32[]{:S(2)}, u32[]{:S(2)}) async-start(bf16[16,64,128]{2,1,0:T(8,128)(2,1)} %broadcast_in_dim.8), calls=%async_computation | async-start | bytes 524288 | tf_op jit(solution)/shard_map/gather_queries/all_to_all | solution.py:28
  11.8 0.0 copy-start.1
  11.8 0.0 copy-start.3
  11.8 1.1 %dynamic-slice_bitcast_fusion = bf16[768,256]{1,0:T(8,128)(2,1)S(1)} fusion(bf16[2,1024,256]{2,1,0:T(8,128)(2,1)} %bitcast.12, s32[]{:T(128)S(6)} %select_n.4), kind=kLoop, calls=%fused_computation | loop fusion | bytes 786436 | tf_op jit(solution)/shard_map/swap_weight/slice | solution.py:186
  12.9 3.3 %collective-permute-start = (bf16[768,256]{1,0:T(8,128)(2,1)S(1)}, bf16[768,256]{1,0:T(8,128)(2,1)S(1)}, u32[]{:S(2)}, u32[]{:S(2)}) collective-permute-start(bf16[768,256]{1,0:T(8,128)(2,1)S(1)} %dynamic-slice_bitcast_fusion), channel_id=1, source_target_pairs={{0,32},{32,0},{1,33},{33,1},{2,34},{34,2},{3,35},{35,3},{4,36},{36... | collective-permute-start | bytes 1179656 | tf_op jit(solution)/shard_map/swap_weight/ppermute | solution.py:186
  16.2 0.0 copy-start.4
  16.2 0.0 copy-start.5
  16.2 0.0 copy-done.2
  16.2 0.0 copy-done.1
  16.2 0.0 copy-done.3
  16.3 0.6 copy-done.4
  16.9 1.6 %suffix_attention.1 = (f32[64,128]{1,0:T(8,128)S(1)}, f32[8,128]{1,0:T(8,128)S(1)}) custom-call(s32[4]{0:T(128)S(1)} %copy-done.4, bf16[64,128]{1,0:T(8,128)(2,1)S(1)} %bitcast.17, bf16[2048,128]{1,0:T(8,128)(2,1)S(1)} %bitcast.14, bf16[2048,128]{1,0:T(8,128)(2,1)S(1)} %bitcast.15), custom_call_target="tpu_custom_call" | custom-call | flops 134217728 | bytes 1048576 | tf_op jit(solution)/shard_map/suffix_attention/pallas_call | solution.py:189
  18.5 3.8 %all-to-all-done.query_ref = bf16[16,64,128]{2,1,0:T(8,128)(2,1)S(1)} async-done(((bf16[16,64,128]{2,1,0:T(8,128)(2,1)}), bf16[16,64,128]{2,1,0:T(8,128)(2,1)S(1)}, u32[]{:S(2)}, u32[]{:S(2)}) %all-to-all-start) | async-done | bytes 262176 | tf_op jit(solution)/shard_map/gather_queries/all_to_all | solution.py:28
  22.3 0.0 copy-done.5
  22.3 0.0 copy-start
  22.3 7.3 %prompt_attention.1 = bf16[16,72,128]{2,1,0:T(8,128)(2,1)} custom-call(bf16[16,64,128]{2,1,0:T(8,128)(2,1)S(1)} %all-to-all-done.query_ref, bf16[4096,128]{1,0:T(8,128)(2,1)S(1)} %bitcast.18, bf16[4096,128]{1,0:T(8,128)(2,1)} %bitcast.19), custom_call_target="tpu_custom_call" | custom-call | flops 2147483648 | bytes 2097152 | tf_op jit(solution)/shard_map/prompt_attention/pallas_call | solution.py:213
  29.7 0.0 collective-permute-done.upper_ref
  29.7 4.3 %all-to-all-start.1 = ((bf16[16,72,128]{2,1,0:T(8,128)(2,1)}), bf16[16,72,128]{2,1,0:T(8,128)(2,1)S(1)}, u32[]{:S(2)}, u32[]{:S(2)}) async-start(bf16[16,72,128]{2,1,0:T(8,128)(2,1)} %prompt_attention.1), calls=%async_computation.1 | async-start | bytes 589824 | tf_op jit(solution)/shard_map/return_partials/all_to_all | solution.py:237
  34.0 0.0 copy-done
  34.0 3.3 %collective-permute-start.1 = (bf16[256,256]{1,0:T(8,128)(2,1)S(1)}, bf16[256,256]{1,0:T(8,128)(2,1)S(1)}, u32[]{:S(2)}, u32[]{:S(2)}) collective-permute-start(bf16[256,256]{1,0:T(8,128)(2,1)S(1)} %dynamic-slice_bitcast_fusion.1), channel_id=1, source_target_pairs={{0,32},{32,0},{1,33},{33,1},{2,34},{34,2},{3,35},{35,3},{4,36},{36... | collective-permute-start | bytes 393224 | tf_op jit(solution)/shard_map/swap_weight/ppermute | solution.py:186
  37.3 6.9 %all-to-all-done.1.back_ref = bf16[16,72,128]{2,1,0:T(8,128)(2,1)S(1)} async-done(((bf16[16,72,128]{2,1,0:T(8,128)(2,1)}), bf16[16,72,128]{2,1,0:T(8,128)(2,1)S(1)}, u32[]{:S(2)}, u32[]{:S(2)}) %all-to-all-start.1) | async-done | bytes 294944 | tf_op jit(solution)/shard_map/return_partials/all_to_all | solution.py:237
  44.2 1.0 %combine.1 = (bf16[64,128]{1,0:T(8,128)(2,1)}, bf16[64,32,128]{2,1,0:T(8,128)(2,1)S(1)}) custom-call(s32[1]{0:T(128)} %bitcast.half_ref, bf16[16,72,128]{2,1,0:T(8,128)(2,1)S(1)} %all-to-all-done.1.back_ref, f32[64,128]{1,0:T(8,128)S(1)} %get-tuple-element.17.numer_ref, f32[8,128]{1,0:T(8,128)S(1)} %get-tuple-element.18.stat_ref), custom_call_target="tpu_custom_call" | custom-call | tf_op jit(solution)/shard_map/combine/pallas_call | solution.py:239
  45.2 0.0 collective-permute-done.1.lower_ref
  45.2 28.8 %all_to_all.20.block_ref = bf16[64,32,128]{2,1,0:T(8,128)(2,1)S(1)} all-to-all(bf16[64,32,128]{2,1,0:T(8,128)(2,1)S(1)} %get-tuple-element.21), channel_id=1, replica_groups=mesh['y'=8,'zl'=2,'x'=4,'core'=2,'zh'=4] {'y','zl','zh'}, dimensions={0} | all-to-all | bytes 1048576 | tf_op jit(solution)/shard_map/gather_attended/all_to_all | solution.py:252
  74.1 0.5 project.1
  74.6 16.1 %all_to_all.21 = bf16[16,32,256]{2,1,0:T(8,128)(2,1)S(1)} all-to-all(bf16[16,32,256]{2,1,0:T(8,128)(2,1)S(1)} %project.1), channel_id=1, replica_groups=mesh['y'=8,'zl'=2,'x'=4,'core'=2,'zh'=4] {'x','core','zl'}, dimensions={0} | all-to-all | bytes 524288 | tf_op jit(solution)/shard_map/sum_heads/all_to_all | solution.py:265
  90.7 0.6 reduce_sum.12
  (1 shorter events, 0.0 us)
Async XLA Ops:
  2.1 14.1 %copy-start.2 = (bf16[4,512,1,128]{3,1,2,0:T(8,128)(2,1)S(1)}, bf16[4,512,1,128]{3,1,2,0:T(8,128)(2,1)}, u32[]{:S(2)}) copy-start(bf16[4,512,1,128]{3,1,2,0:T(8,128)(2,1)} %param.11) | copy-start | bytes 1572868
  2.1 20.2 %all-to-all-start = ((bf16[16,64,128]{2,1,0:T(8,128)(2,1)}), bf16[16,64,128]{2,1,0:T(8,128)(2,1)S(1)}, u32[]{:S(2)}, u32[]{:S(2)}) async-start(bf16[16,64,128]{2,1,0:T(8,128)(2,1)} %broadcast_in_dim.8), calls=%async_computation | async-start | bytes 524288 | tf_op jit(solution)/shard_map/gather_queries/all_to_all | solution.py:28
  11.8 4.4 %copy-start.1 = (bf16[4,512,1,128]{3,1,2,0:T(8,128)(2,1)S(1)}, bf16[4,512,1,128]{3,1,2,0:T(8,128)(2,1)}, u32[]{:S(2)}) copy-start(bf16[4,512,1,128]{3,1,2,0:T(8,128)(2,1)} %param.10) | copy-start | bytes 1572868
  11.8 4.4 %copy-start.3 = (bf16[4,16,128]{2,1,0:T(8,128)(2,1)S(1)}, bf16[4,16,128]{2,1,0:T(8,128)(2,1)}, u32[]{:S(2)}) copy-start(bf16[4,16,128]{2,1,0:T(8,128)(2,1)} %param.7) | copy-start | bytes 49156
  12.9 16.7 %collective-permute-start = (bf16[768,256]{1,0:T(8,128)(2,1)S(1)}, bf16[768,256]{1,0:T(8,128)(2,1)S(1)}, u32[]{:S(2)}, u32[]{:S(2)}) collective-permute-start(bf16[768,256]{1,0:T(8,128)(2,1)S(1)} %dynamic-slice_bitcast_fusion), channel_id=1, source_target_pairs={{0,32},{32,0},{1,33},{33,1},{2,34},{34,2},{3,35},{35,3},{4,36},{36... | collective-permute-start | bytes 1179656 | tf_op jit(solution)/shard_map/swap_weight/ppermute | solution.py:186
  16.2 0.7 copy-start.4
  16.2 6.1 %copy-start.5 = (bf16[4096,1,128]{2,0,1:T(8,128)(2,1)S(1)}, bf16[4096,1,128]{2,0,1:T(8,128)(2,1)}, u32[]{:S(2)}) copy-start(bf16[4096,1,128]{2,0,1:T(8,128)(2,1)} %param.8) | copy-start | bytes 3145732
  22.3 11.6 %copy-start = (bf16[2048,256]{1,0:T(8,128)(2,1)S(1)}, bf16[2048,256]{1,0:T(8,128)(2,1)}, u32[]{:S(2)}) copy-start(bf16[2048,256]{1,0:T(8,128)(2,1)} %weight_ref.1) | copy-start | bytes 3145732
  29.7 14.5 %all-to-all-start.1 = ((bf16[16,72,128]{2,1,0:T(8,128)(2,1)}), bf16[16,72,128]{2,1,0:T(8,128)(2,1)S(1)}, u32[]{:S(2)}, u32[]{:S(2)}) async-start(bf16[16,72,128]{2,1,0:T(8,128)(2,1)} %prompt_attention.1), calls=%async_computation.1 | async-start | bytes 589824 | tf_op jit(solution)/shard_map/return_partials/all_to_all | solution.py:237
  34.0 11.2 %collective-permute-start.1 = (bf16[256,256]{1,0:T(8,128)(2,1)S(1)}, bf16[256,256]{1,0:T(8,128)(2,1)S(1)}, u32[]{:S(2)}, u32[]{:S(2)}) collective-permute-start(bf16[256,256]{1,0:T(8,128)(2,1)S(1)} %dynamic-slice_bitcast_fusion.1), channel_id=1, source_target_pairs={{0,32},{32,0},{1,33},{33,1},{2,34},{34,2},{3,35},{35,3},{4,36},{36... | collective-permute-start | bytes 393224 | tf_op jit(solution)/shard_map/swap_weight/ppermute | solution.py:186

commit v5 on v4

--- a/solution.py
+++ b/solution.py
@@ -14,6 +14,7 @@
 KVH = ("x", "core")
 REP = ("zh",)
 VMEM = pl.BlockSpec(memory_space=pltpu.VMEM)
+HBM = pl.BlockSpec(memory_space=pltpu.HBM)
 SMEM = pl.BlockSpec(memory_space=pltpu.SMEM)
 LAST_WITH_LAST = (((1,), (1,)), ((), ()))
 FIRST_WITH_FIRST = (((0,), (0,)), ((), ()))
@@ -22,10 +23,6 @@
 
 def base_two(head_dim):
     return math.log2(math.e) / math.sqrt(head_dim)
-
-
-def gathered(copies, axes):
-    return lax.all_to_all(copies, axes, 0, 0, tiled=False)
 
 
 def suffix_kernel(len_ref, query_ref, key_ref, value_ref, numer_ref, stat_ref, *, conts):
@@ -133,7 +130,11 @@
         copies_ref[place] = parts[place // rep % 2]
 
 
-def project_kernel(half_ref, block_ref, weight_ref, upper_ref, lower_ref, out_ref, wide_ref):
+def project_kernel(
+    half_ref, block_ref, weight_ref, upper_ref, lower_ref, home_ref, out_ref, home_hbm, wide_ref, home_sem
+):
+    home_copy = pltpu.make_async_copy(home_ref, home_hbm, home_sem)
+    home_copy.start()
     places, block_rows, head_dim = block_ref.shape
     wide_ref[...] = block_ref[...].reshape(places * block_rows, head_dim).astype(jnp.float32)
     heads = weight_ref.shape[0] // (2 * head_dim)
@@ -158,6 +159,7 @@
         rows = slice(group * out_rows, (group + 1) * out_rows)
         out_ref[2 * group + half] = own[rows]
         out_ref[2 * group + 1 - half] = other[rows]
+    home_copy.wait()
 
 
 def body(queries, prompt_keys, prompt_values, suffix_keys, suffix_values, suffix_len, out_weight):
@@ -175,9 +177,8 @@
     query_rows = queries.reshape(rows, head_dim)
 
     with jax.named_scope("gather_queries"):
-        visiting = gathered(
-            jnp.broadcast_to(query_rows[None], (ctx, rows, head_dim)), CTX
-        )
+        copies = jnp.broadcast_to(query_rows[None], (ctx, rows, head_dim))
+        visiting = lax.all_to_all(copies, CTX, 0, 0, tiled=False)
     with jax.named_scope("swap_weight"):
         halves = out_weight.reshape(2, depth // 2, width)
         given = lax.dynamic_index_in_dim(halves, 1 - half, 0, keepdims=False)
@@ -212,7 +213,7 @@
     with jax.named_scope("prompt_attention"):
         sent = pl.pallas_call(
             prompt_kernel,
-            in_specs=[VMEM, VMEM, pl.BlockSpec(memory_space=pltpu.HBM)],
+            in_specs=[VMEM, VMEM, HBM],
             out_specs=VMEM,
             scratch_shapes=[
                 pltpu.VMEM((tokens, head_dim), jnp.bfloat16),
@@ -251,16 +252,20 @@
     with jax.named_scope("gather_attended"):
         everyone = lax.all_to_all(copies, CTX + REP, 0, 0, tiled=False)
     with jax.named_scope("project"):
-        terms = pl.pallas_call(
+        terms, attended = pl.pallas_call(
             project_kernel,
-            in_specs=[SMEM, VMEM, VMEM, VMEM, VMEM],
-            out_specs=VMEM,
-            out_shape=jax.ShapeDtypeStruct(
-                (2 * kvh, ctx * rep * conts // kvh, width), jnp.bfloat16
-            ),
-            scratch_shapes=[pltpu.VMEM((ctx * rep * rows // 2, head_dim), jnp.float32)],
+            in_specs=[SMEM] + [VMEM] * 5,
+            out_specs=[VMEM, HBM],
+            out_shape=[
+                jax.ShapeDtypeStruct((2 * kvh, ctx * rep * conts // kvh, width), jnp.bfloat16),
+                jax.ShapeDtypeStruct((rows, head_dim), jnp.bfloat16),
+            ],
+            scratch_shapes=[
+                pltpu.VMEM((ctx * rep * rows // 2, head_dim), jnp.float32),
+                pltpu.SemaphoreType.DMA,
+            ],
             compiler_params=small,
-        )(half.reshape(1), everyone, out_weight, taken[0], taken[1])
+        )(half.reshape(1), everyone, out_weight, taken[0], taken[1], attended)
     with jax.named_scope("sum_heads"):
         parts = lax.all_to_all(terms, KVH + ("zl",), 0, 0, tiled=False)
         projected = jnp.sum(parts.astype(jnp.float32), axis=0).astype(jnp.bfloat16)

time: 91.9 us -> 91.6 us (level)
  transfers between devices with their start and end apart: 4 -> 4, of which waited for: 2 -> 2; matrix products, arithmetic and copies ran while one was open for 1% -> 1% of each run, Pallas kernels for 11% -> 10%
where the time goes in v5:
time: 91.6 us; the launch traced here: 91.1 us
  blocking collectives  45.2 us (49%)
  starting transfers between devices  20.5 us (22%)
  waiting for transfers between devices  10.8 us (12%)
  Pallas kernels  10 us (11%)
  local copies, waits for them, and re-layouts  3.21 us (4%)
    all_to_all x1, blocking collectives, body(): everyone = lax.all_to_all(copies, CTX + REP, 0, 0, tiled=False)  28.8 us
    all_to_all x1, blocking collectives, body(): parts = lax.all_to_all(terms, KVH + ('zl',), 0, 0, tiled=False)  16.3 us
    all_to_all x1, starting transfers between devices, body(): visiting = lax.all_to_all(copies, CTX, 0, 0, tiled=False)  9.69 us
    pallas_call x1, Pallas kernels, body(): pl.pallas_call(prompt_kernel, in_specs=[VMEM, VMEM, HBM], out_specs=VMEM,...  7.36 us
    all_to_all x1, waiting for transfers between devices, body(): back = lax.all_to_all(sent, CTX, 0, 0, tiled=False)  6.92 us
    ppermute x2, starting transfers between devices, body(): lax.ppermute(part, 'zl', [(0, 1), (1, 0)])  6.54 us
    all_to_all x1, starting transfers between devices, body(): back = lax.all_to_all(sent, CTX, 0, 0, tiled=False)  4.26 us
    all_to_all x1, waiting for transfers between devices, body(): visiting = lax.all_to_all(copies, CTX, 0, 0, tiled=False)  3.84 us
  transfers between devices with their start and end apart: 4, of which 2 were waited for; matrix products, arithmetic and copies ran while one was open for 1% of the time, Pallas kernels for 10%

profile of v5, /device:TPU:1, one launch (start us, length us, event | category | flops | bytes accessed | tf_op | source)
XLA Modules:
  0.0 91.1 jit_solution(15269759812044484295)
XLA Ops:
  0.6 1.5 %broadcast_in_dim.8 = bf16[16,64,128]{2,1,0:T(8,128)(2,1)} broadcast(bf16[64,128]{1,0:T(8,128)(2,1)} %bitcast.16), dimensions={1,2} | broadcast | bytes 278528 | tf_op jit(solution)/shard_map/gather_queries/broadcast_in_dim | solution.py:180
  2.1 0.0 copy-start.2
  2.1 9.7 %all-to-all-start = ((bf16[16,64,128]{2,1,0:T(8,128)(2,1)}), bf16[16,64,128]{2,1,0:T(8,128)(2,1)S(1)}, u32[]{:S(2)}, u32[]{:S(2)}) async-start(bf16[16,64,128]{2,1,0:T(8,128)(2,1)} %broadcast_in_dim.8), calls=%async_computation | async-start | bytes 524288 | tf_op jit(solution)/shard_map/gather_queries/all_to_all | solution.py:181
  11.8 0.0 copy-start.1
  11.8 0.0 copy-start.3
  11.8 1.1 %dynamic-slice_bitcast_fusion = bf16[768,256]{1,0:T(8,128)(2,1)S(1)} fusion(bf16[2,1024,256]{2,1,0:T(8,128)(2,1)} %bitcast.12, s32[]{:T(128)S(6)} %select_n.4), kind=kLoop, calls=%fused_computation | loop fusion | bytes 786436 | tf_op jit(solution)/shard_map/swap_weight/slice | solution.py:187
  12.9 3.3 %collective-permute-start = (bf16[768,256]{1,0:T(8,128)(2,1)S(1)}, bf16[768,256]{1,0:T(8,128)(2,1)S(1)}, u32[]{:S(2)}, u32[]{:S(2)}) collective-permute-start(bf16[768,256]{1,0:T(8,128)(2,1)S(1)} %dynamic-slice_bitcast_fusion), channel_id=1, source_target_pairs={{0,32},{32,0},{1,33},{33,1},{2,34},{34,2},{3,35},{35,3},{4,36},{36... | collective-permute-start | bytes 1179656 | tf_op jit(solution)/shard_map/swap_weight/ppermute | solution.py:187
  16.2 0.0 copy-start.4
  16.2 0.0 copy-start.5
  16.2 0.0 copy-done.2
  16.2 0.0 copy-done.1
  16.2 0.0 copy-done.3
  16.3 0.6 copy-done.4
  16.9 1.6 %suffix_attention.1 = (f32[64,128]{1,0:T(8,128)S(1)}, f32[8,128]{1,0:T(8,128)S(1)}) custom-call(s32[4]{0:T(128)S(1)} %copy-done.4, bf16[64,128]{1,0:T(8,128)(2,1)S(1)} %bitcast.17, bf16[2048,128]{1,0:T(8,128)(2,1)S(1)} %bitcast.14, bf16[2048,128]{1,0:T(8,128)(2,1)S(1)} %bitcast.15), custom_call_target="tpu_custom_call" | custom-call | flops 134217728 | bytes 1048576 | tf_op jit(solution)/shard_map/suffix_attention/pallas_call | solution.py:190
  18.5 3.8 %all-to-all-done.query_ref = bf16[16,64,128]{2,1,0:T(8,128)(2,1)S(1)} async-done(((bf16[16,64,128]{2,1,0:T(8,128)(2,1)}), bf16[16,64,128]{2,1,0:T(8,128)(2,1)S(1)}, u32[]{:S(2)}, u32[]{:S(2)}) %all-to-all-start) | async-done | bytes 262176 | tf_op jit(solution)/shard_map/gather_queries/all_to_all | solution.py:181
  22.3 0.0 copy-done.5
  22.3 0.0 copy-start
  22.3 7.4 %prompt_attention.1 = bf16[16,72,128]{2,1,0:T(8,128)(2,1)} custom-call(bf16[16,64,128]{2,1,0:T(8,128)(2,1)S(1)} %all-to-all-done.query_ref, bf16[4096,128]{1,0:T(8,128)(2,1)S(1)} %bitcast.18, bf16[4096,128]{1,0:T(8,128)(2,1)} %bitcast.19), custom_call_target="tpu_custom_call" | custom-call | flops 2147483648 | bytes 2097152 | tf_op jit(solution)/shard_map/prompt_attention/pallas_call | solution.py:214
  29.7 0.0 collective-permute-done.upper_ref
  29.7 4.3 %all-to-all-start.1 = ((bf16[16,72,128]{2,1,0:T(8,128)(2,1)}), bf16[16,72,128]{2,1,0:T(8,128)(2,1)S(1)}, u32[]{:S(2)}, u32[]{:S(2)}) async-start(bf16[16,72,128]{2,1,0:T(8,128)(2,1)} %prompt_attention.1), calls=%async_computation.1 | async-start | bytes 589824 | tf_op jit(solution)/shard_map/return_partials/all_to_all | solution.py:238
  34.0 0.0 copy-done
  34.0 3.3 %collective-permute-start.1 = (bf16[256,256]{1,0:T(8,128)(2,1)S(1)}, bf16[256,256]{1,0:T(8,128)(2,1)S(1)}, u32[]{:S(2)}, u32[]{:S(2)}) collective-permute-start(bf16[256,256]{1,0:T(8,128)(2,1)S(1)} %dynamic-slice_bitcast_fusion.1), channel_id=1, source_target_pairs={{0,32},{32,0},{1,33},{33,1},{2,34},{34,2},{3,35},{35,3},{4,36},{36... | collective-permute-start | bytes 393224 | tf_op jit(solution)/shard_map/swap_weight/ppermute | solution.py:187
  37.3 6.9 %all-to-all-done.1.back_ref = bf16[16,72,128]{2,1,0:T(8,128)(2,1)S(1)} async-done(((bf16[16,72,128]{2,1,0:T(8,128)(2,1)}), bf16[16,72,128]{2,1,0:T(8,128)(2,1)S(1)}, u32[]{:S(2)}, u32[]{:S(2)}) %all-to-all-start.1) | async-done | bytes 294944 | tf_op jit(solution)/shard_map/return_partials/all_to_all | solution.py:238
  44.2 0.4 combine.1
  44.6 0.0 collective-permute-done.1.lower_ref
  44.6 28.8 %all_to_all.20.block_ref = bf16[64,32,128]{2,1,0:T(8,128)(2,1)S(1)} all-to-all(bf16[64,32,128]{2,1,0:T(8,128)(2,1)S(1)} %get-tuple-element.22), channel_id=1, replica_groups=mesh['y'=8,'zl'=2,'x'=4,'core'=2,'zh'=4] {'y','zl','zh'}, dimensions={0} | all-to-all | bytes 1048576 | tf_op jit(solution)/shard_map/gather_attended/all_to_all | solution.py:253
  73.5 0.6 project.1
  74.1 16.3 %all_to_all.21 = bf16[16,32,256]{2,1,0:T(8,128)(2,1)S(1)} all-to-all(bf16[16,32,256]{2,1,0:T(8,128)(2,1)S(1)} %get-tuple-element.27), channel_id=1, replica_groups=mesh['y'=8,'zl'=2,'x'=4,'core'=2,'zh'=4] {'x','core','zl'}, dimensions={0} | all-to-all | bytes 524288 | tf_op jit(solution)/shard_map/sum_heads/all_to_all | solution.py:270
  90.5 0.6 reduce_sum.12
  (1 shorter events, 0.0 us)
Async XLA Ops:
  2.1 14.1 %copy-start.2 = (bf16[4,512,1,128]{3,1,2,0:T(8,128)(2,1)S(1)}, bf16[4,512,1,128]{3,1,2,0:T(8,128)(2,1)}, u32[]{:S(2)}) copy-start(bf16[4,512,1,128]{3,1,2,0:T(8,128)(2,1)} %param.11) | copy-start | bytes 1572868
  2.1 20.2 %all-to-all-start = ((bf16[16,64,128]{2,1,0:T(8,128)(2,1)}), bf16[16,64,128]{2,1,0:T(8,128)(2,1)S(1)}, u32[]{:S(2)}, u32[]{:S(2)}) async-start(bf16[16,64,128]{2,1,0:T(8,128)(2,1)} %broadcast_in_dim.8), calls=%async_computation | async-start | bytes 524288 | tf_op jit(solution)/shard_map/gather_queries/all_to_all | solution.py:181
  11.8 4.4 %copy-start.1 = (bf16[4,512,1,128]{3,1,2,0:T(8,128)(2,1)S(1)}, bf16[4,512,1,128]{3,1,2,0:T(8,128)(2,1)}, u32[]{:S(2)}) copy-start(bf16[4,512,1,128]{3,1,2,0:T(8,128)(2,1)} %param.10) | copy-start | bytes 1572868
  11.8 4.4 %copy-start.3 = (bf16[4,16,128]{2,1,0:T(8,128)(2,1)S(1)}, bf16[4,16,128]{2,1,0:T(8,128)(2,1)}, u32[]{:S(2)}) copy-start(bf16[4,16,128]{2,1,0:T(8,128)(2,1)} %param.7) | copy-start | bytes 49156
  12.9 16.8 %collective-permute-start = (bf16[768,256]{1,0:T(8,128)(2,1)S(1)}, bf16[768,256]{1,0:T(8,128)(2,1)S(1)}, u32[]{:S(2)}, u32[]{:S(2)}) collective-permute-start(bf16[768,256]{1,0:T(8,128)(2,1)S(1)} %dynamic-slice_bitcast_fusion), channel_id=1, source_target_pairs={{0,32},{32,0},{1,33},{33,1},{2,34},{34,2},{3,35},{35,3},{4,36},{36... | collective-permute-start | bytes 1179656 | tf_op jit(solution)/shard_map/swap_weight/ppermute | solution.py:187
  16.2 0.7 copy-start.4
  16.2 6.1 %copy-start.5 = (bf16[4096,1,128]{2,0,1:T(8,128)(2,1)S(1)}, bf16[4096,1,128]{2,0,1:T(8,128)(2,1)}, u32[]{:S(2)}) copy-start(bf16[4096,1,128]{2,0,1:T(8,128)(2,1)} %param.8) | copy-start | bytes 3145732
  22.3 11.6 %copy-start = (bf16[2048,256]{1,0:T(8,128)(2,1)S(1)}, bf16[2048,256]{1,0:T(8,128)(2,1)}, u32[]{:S(2)}) copy-start(bf16[2048,256]{1,0:T(8,128)(2,1)} %weight_ref.1) | copy-start | bytes 3145732
  29.7 14.5 %all-to-all-start.1 = ((bf16[16,72,128]{2,1,0:T(8,128)(2,1)}), bf16[16,72,128]{2,1,0:T(8,128)(2,1)S(1)}, u32[]{:S(2)}, u32[]{:S(2)}) async-start(bf16[16,72,128]{2,1,0:T(8,128)(2,1)} %prompt_attention.1), calls=%async_computation.1 | async-start | bytes 589824 | tf_op jit(solution)/shard_map/return_partials/all_to_all | solution.py:238
  34.0 10.6 %collective-permute-start.1 = (bf16[256,256]{1,0:T(8,128)(2,1)S(1)}, bf16[256,256]{1,0:T(8,128)(2,1)S(1)}, u32[]{:S(2)}, u32[]{:S(2)}) collective-permute-start(bf16[256,256]{1,0:T(8,128)(2,1)S(1)} %dynamic-slice_bitcast_fusion.1), channel_id=1, source_target_pairs={{0,32},{32,0},{1,33},{33,1},{2,34},{34,2},{3,35},{35,3},{4,36},{36... | collective-permute-start | bytes 393224 | tf_op jit(solution)/shard_map/swap_weight/ppermute | solution.py:187

commit v6 on v5

--- a/solution.py
+++ b/solution.py
@@ -3,6 +3,7 @@
 
 import jax
 import jax.numpy as jnp
+import numpy as np
 from jax import lax
 from jax.experimental import pallas as pl
 from jax.experimental.pallas import tpu as pltpu
@@ -10,15 +11,23 @@
 from jax.sharding import PartitionSpec as P
 
 FAR_BELOW = -1e30
-CTX = ("y", "zl")
+CTX = ("y4", "y2", "y1", "zl")
 KVH = ("x", "core")
-REP = ("zh",)
+REP = ("z4", "z2")
+CTX_ORDER = ("zl", "y4", "y1", "y2")
+ALL_ORDER = ("y4", "y2", "y1", "z4", "z2", "zl")
 VMEM = pl.BlockSpec(memory_space=pltpu.VMEM)
 HBM = pl.BlockSpec(memory_space=pltpu.HBM)
 SMEM = pl.BlockSpec(memory_space=pltpu.SMEM)
 LAST_WITH_LAST = (((1,), (1,)), ((), ()))
 FIRST_WITH_FIRST = (((0,), (0,)), ((), ()))
 STAT_ROWS = 8
+
+
+def home_places(sizes):
+    names = CTX + REP
+    grid = np.arange(math.prod(sizes)).reshape(sizes)
+    return grid.transpose([names.index(name) for name in ALL_ORDER]).reshape(-1).tolist()
 
 
 def base_two(head_dim):
@@ -96,7 +105,9 @@
         out_ref[block, block_rows:, :] = stats[:, tile * head_dim : (tile + 1) * head_dim]
 
 
-def combine_kernel(half_ref, back_ref, numer_ref, stat_ref, out_ref, copies_ref, spread_ref, *, rep):
+def combine_kernel(
+    half_ref, back_ref, numer_ref, stat_ref, out_ref, copies_ref, spread_ref, *, sides
+):
     blocks, _, head_dim = back_ref.shape
     rows = out_ref.shape[0]
     stats = back_ref[:, rows:, :].astype(jnp.float32)
@@ -126,17 +137,29 @@
     parts = [
         slabs[:, part].reshape(rows // 2, head_dim).astype(jnp.bfloat16) for part in range(2)
     ]
-    for place in range(copies_ref.shape[0]):
-        copies_ref[place] = parts[place // rep % 2]
+    for place, side in enumerate(sides):
+        copies_ref[place] = parts[side]
 
 
 def project_kernel(
-    half_ref, block_ref, weight_ref, upper_ref, lower_ref, home_ref, out_ref, home_hbm, wide_ref, home_sem
+    half_ref,
+    block_ref,
+    weight_ref,
+    upper_ref,
+    lower_ref,
+    home_ref,
+    out_ref,
+    home_hbm,
+    wide_ref,
+    home_sem,
+    *,
+    homes,
 ):
     home_copy = pltpu.make_async_copy(home_ref, home_hbm, home_sem)
     home_copy.start()
     places, block_rows, head_dim = block_ref.shape
-    wide_ref[...] = block_ref[...].reshape(places * block_rows, head_dim).astype(jnp.float32)
+    for place, home in enumerate(homes):
+        wide_ref[pl.ds(home * block_rows, block_rows), :] = block_ref[place].astype(jnp.float32)
     heads = weight_ref.shape[0] // (2 * head_dim)
     conts = places * block_rows // heads
     left = jnp.concatenate(
@@ -169,6 +192,7 @@
     rep = lax.axis_size(REP)
     kvh = lax.axis_size(KVH)
     half = lax.axis_index("zl")
+    homes = home_places([lax.axis_size(name) for name in CTX + REP])
     tokens = prompt_keys.shape[0]
     slots = suffix_keys.shape[1]
     depth, width = out_weight.shape
@@ -178,7 +202,7 @@
 
     with jax.named_scope("gather_queries"):
         copies = jnp.broadcast_to(query_rows[None], (ctx, rows, head_dim))
-        visiting = lax.all_to_all(copies, CTX, 0, 0, tiled=False)
+        visiting = lax.all_to_all(copies, CTX_ORDER, 0, 0, tiled=False)
     with jax.named_scope("swap_weight"):
         halves = out_weight.reshape(2, depth // 2, width)
         given = lax.dynamic_index_in_dim(halves, 1 - half, 0, keepdims=False)
@@ -235,10 +259,10 @@
         )
     sent, taken[0] = lax.optimization_barrier((sent, taken[0]))
     with jax.named_scope("return_partials"):
-        back = lax.all_to_all(sent, CTX, 0, 0, tiled=False)
+        back = lax.all_to_all(sent, CTX_ORDER, 0, 0, tiled=False)
     with jax.named_scope("combine"):
         attended, copies = pl.pallas_call(
-            functools.partial(combine_kernel, rep=rep),
+            functools.partial(combine_kernel, sides=[home // rep % 2 for home in homes]),
             in_specs=[SMEM, VMEM, VMEM, VMEM],
             out_specs=[VMEM, VMEM],
             out_shape=[
@@ -247,13 +271,13 @@
             ],
             scratch_shapes=[pltpu.VMEM((head_dim, head_dim), jnp.float32)],
             compiler_params=small,
-        )(half.reshape(1), back, home_numer, home_stat)
+        )(lax.axis_index(CTX_ORDER[-1]).reshape(1), back, home_numer, home_stat)
     copies, taken[1] = lax.optimization_barrier((copies, taken[1]))
     with jax.named_scope("gather_attended"):
-        everyone = lax.all_to_all(copies, CTX + REP, 0, 0, tiled=False)
+        everyone = lax.all_to_all(copies, ALL_ORDER, 0, 0, tiled=False)
     with jax.named_scope("project"):
         terms, attended = pl.pallas_call(
-            project_kernel,
+            functools.partial(project_kernel, homes=homes),
             in_specs=[SMEM] + [VMEM] * 5,
             out_specs=[VMEM, HBM],
             out_shape=[
@@ -275,7 +299,8 @@
 def solution(mesh):
     ctx, kvh, rep = (mesh.shape[name] for name in ("ctx", "kvh", "rep"))
     fine = Mesh(
-        mesh.devices.reshape(ctx // 2, 2, kvh // 2, 2, rep), ("y", "zl", "x", "core", "zh")
+        mesh.devices.reshape(2, 2, ctx // 8, 2, kvh // 2, 2, 2, rep // 2),
+        CTX + KVH + REP,
     )
     groups = CTX + REP
     in_specs = (

time: 91.6 us -> 89.4 us (0.976)
  waiting for transfers between devices: 10.8 us -> 6.55 us
  starting transfers between devices: 20.5 us -> 22.4 us
    all_to_all x2, waiting for transfers between devices: 10.8 us -> 6.54 us  [the longest x1 5.42 us: body(): back = lax.all_to_all(sent, CTX_ORDER, 0, 0, tiled=False)]
    all_to_all x2, starting transfers between devices: 13.9 us -> 15.9 us  [the longest x1 9.69 us: body(): visiting = lax.all_to_all(copies, CTX_ORDER, 0, 0, tiled=False)]
  transfers between devices with their start and end apart: 4 -> 4, of which waited for: 2 -> 2; matrix products, arithmetic and copies ran while one was open for 1% -> 1% of each run, Pallas kernels for 10% -> 11%
where the time goes in v6:
time: 89.4 us; the launch traced here: 88.9 us
  blocking collectives  45.2 us (51%)
  starting transfers between devices  22.4 us (25%)
  Pallas kernels  10.1 us (11%)
  waiting for transfers between devices  6.55 us (7%)
  local copies, waits for them, and re-layouts  3.21 us (4%)
    all_to_all x1, blocking collectives, body(): everyone = lax.all_to_all(copies, ALL_ORDER, 0, 0, tiled=False)  28.3 us
    all_to_all x1, blocking collectives, body(): parts = lax.all_to_all(terms, KVH + ('zl',), 0, 0, tiled=False)  16.9 us
    all_to_all x1, starting transfers between devices, body(): visiting = lax.all_to_all(copies, CTX_ORDER, 0, 0, tiled=False)  9.69 us
    pallas_call x1, Pallas kernels, body(): pl.pallas_call(prompt_kernel, in_specs=[VMEM, VMEM, HBM], out_specs=VMEM,...  7.36 us
    ppermute x2, starting transfers between devices, body(): lax.ppermute(part, 'zl', [(0, 1), (1, 0)])  6.55 us
    all_to_all x1, starting transfers between devices, body(): back = lax.all_to_all(sent, CTX_ORDER, 0, 0, tiled=False)  6.2 us
    all_to_all x1, waiting for transfers between devices, body(): back = lax.all_to_all(sent, CTX_ORDER, 0, 0, tiled=False)  5.42 us
  transfers between devices with their start and end apart: 4, of which 2 were waited for; matrix products, arithmetic and copies ran while one was open for 1% of the time, Pallas kernels for 11%

profile of v6, /device:TPU:1, one launch (start us, length us, event | category | flops | bytes accessed | tf_op | source)
XLA Modules:
  0.0 88.9 jit_solution(12219172488958674519)
XLA Ops:
  0.6 1.5 %broadcast_in_dim.8 = bf16[16,64,128]{2,1,0:T(8,128)(2,1)} broadcast(bf16[64,128]{1,0:T(8,128)(2,1)} %bitcast.17), dimensions={1,2} | broadcast | bytes 278528 | tf_op jit(solution)/shard_map/gather_queries/broadcast_in_dim | solution.py:204
  2.1 0.0 copy-start.2
  2.1 9.7 %all-to-all-start = ((bf16[16,64,128]{2,1,0:T(8,128)(2,1)}), bf16[16,64,128]{2,1,0:T(8,128)(2,1)S(1)}, u32[]{:S(2)}, u32[]{:S(2)}) async-start(bf16[16,64,128]{2,1,0:T(8,128)(2,1)} %broadcast_in_dim.8), calls=%async_computation | async-start | bytes 524288 | tf_op jit(solution)/shard_map/gather_queries/all_to_all | solution.py:205
  11.8 0.0 copy-start.1
  11.8 0.0 copy-start.3
  11.8 1.1 %dynamic-slice_bitcast_fusion = bf16[768,256]{1,0:T(8,128)(2,1)S(1)} fusion(bf16[2,1024,256]{2,1,0:T(8,128)(2,1)} %bitcast.13, s32[]{:T(128)S(6)} %select_n.4), kind=kLoop, calls=%fused_computation | loop fusion | bytes 786436 | tf_op jit(solution)/shard_map/swap_weight/slice | solution.py:211
  12.9 3.3 %collective-permute-start = (bf16[768,256]{1,0:T(8,128)(2,1)S(1)}, bf16[768,256]{1,0:T(8,128)(2,1)S(1)}, u32[]{:S(2)}, u32[]{:S(2)}) collective-permute-start(bf16[768,256]{1,0:T(8,128)(2,1)S(1)} %dynamic-slice_bitcast_fusion), channel_id=1, source_target_pairs={{0,32},{32,0},{1,33},{33,1},{2,34},{34,2},{3,35},{35,3},{4,36},{36... | collective-permute-start | bytes 1179656 | tf_op jit(solution)/shard_map/swap_weight/ppermute | solution.py:211
  16.2 0.0 copy-start.4
  16.2 0.0 copy-start.5
  16.2 0.0 copy-done.2
  16.2 0.0 copy-done.1
  16.2 0.0 copy-done.3
  16.3 0.6 copy-done.4
  16.9 1.6 %suffix_attention.1 = (f32[64,128]{1,0:T(8,128)S(1)}, f32[8,128]{1,0:T(8,128)S(1)}) custom-call(s32[4]{0:T(128)S(1)} %copy-done.4, bf16[64,128]{1,0:T(8,128)(2,1)S(1)} %bitcast.18, bf16[2048,128]{1,0:T(8,128)(2,1)S(1)} %bitcast.15, bf16[2048,128]{1,0:T(8,128)(2,1)S(1)} %bitcast.16), custom_call_target="tpu_custom_call" | custom-call | flops 134217728 | bytes 1048576 | tf_op jit(solution)/shard_map/suffix_attention/pallas_call | solution.py:214
  18.5 1.1 %all-to-all-done.query_ref = bf16[16,64,128]{2,1,0:T(8,128)(2,1)S(1)} async-done(((bf16[16,64,128]{2,1,0:T(8,128)(2,1)}), bf16[16,64,128]{2,1,0:T(8,128)(2,1)S(1)}, u32[]{:S(2)}, u32[]{:S(2)}) %all-to-all-start) | async-done | bytes 262176 | tf_op jit(solution)/shard_map/gather_queries/all_to_all | solution.py:205
  19.6 0.0 copy-done.5
  19.6 0.0 copy-start
  19.6 7.4 %prompt_attention.1 = bf16[16,72,128]{2,1,0:T(8,128)(2,1)} custom-call(bf16[16,64,128]{2,1,0:T(8,128)(2,1)S(1)} %all-to-all-done.query_ref, bf16[4096,128]{1,0:T(8,128)(2,1)S(1)} %bitcast.19, bf16[4096,128]{1,0:T(8,128)(2,1)} %bitcast.20), custom_call_target="tpu_custom_call" | custom-call | flops 2147483648 | bytes 2097152 | tf_op jit(solution)/shard_map/prompt_attention/pallas_call | solution.py:238
  27.0 0.0 collective-permute-done.upper_ref
  27.0 6.2 %all-to-all-start.1 = ((bf16[16,72,128]{2,1,0:T(8,128)(2,1)}), bf16[16,72,128]{2,1,0:T(8,128)(2,1)S(1)}, u32[]{:S(2)}, u32[]{:S(2)}) async-start(bf16[16,72,128]{2,1,0:T(8,128)(2,1)} %prompt_attention.1), calls=%async_computation.1 | async-start | bytes 589824 | tf_op jit(solution)/shard_map/return_partials/all_to_all | solution.py:262
  33.2 0.0 copy-done
  33.2 3.3 %collective-permute-start.1 = (bf16[256,256]{1,0:T(8,128)(2,1)S(1)}, bf16[256,256]{1,0:T(8,128)(2,1)S(1)}, u32[]{:S(2)}, u32[]{:S(2)}) collective-permute-start(bf16[256,256]{1,0:T(8,128)(2,1)S(1)} %dynamic-slice_bitcast_fusion.1), channel_id=1, source_target_pairs={{0,32},{32,0},{1,33},{33,1},{2,34},{34,2},{3,35},{35,3},{4,36},{36... | collective-permute-start | bytes 393224 | tf_op jit(solution)/shard_map/swap_weight/ppermute | solution.py:211
  36.5 5.4 %all-to-all-done.1.back_ref = bf16[16,72,128]{2,1,0:T(8,128)(2,1)S(1)} async-done(((bf16[16,72,128]{2,1,0:T(8,128)(2,1)}), bf16[16,72,128]{2,1,0:T(8,128)(2,1)S(1)}, u32[]{:S(2)}, u32[]{:S(2)}) %all-to-all-start.1) | async-done | bytes 294944 | tf_op jit(solution)/shard_map/return_partials/all_to_all | solution.py:262
  41.9 0.4 combine.1
  42.4 0.0 collective-permute-done.1.lower_ref
  42.4 28.3 %all_to_all.20.block_ref = bf16[64,32,128]{2,1,0:T(8,128)(2,1)S(1)} all-to-all(bf16[64,32,128]{2,1,0:T(8,128)(2,1)S(1)} %get-tuple-element.22), channel_id=1, replica_groups=mesh['y4'=2,'y2'=2,'y1'=2,'zl'=2,'x'=4,'core'=2,'z4'=2,'z2'=2] {'y4','y2..., dimensions={0} | all-to-all | bytes 1048576 | tf_op jit(solution)/shard_map/gather_attended/all_to_all | solution.py:277
  70.7 0.6 project.1
  71.4 16.9 %all_to_all.21 = bf16[16,32,256]{2,1,0:T(8,128)(2,1)S(1)} all-to-all(bf16[16,32,256]{2,1,0:T(8,128)(2,1)S(1)} %get-tuple-element.27), channel_id=1, replica_groups=mesh['y4'=2,'y2'=2,'y1'=2,'zl'=2,'x'=4,'core'=2,'z4'=2,'z2'=2] {'x','cor..., dimensions={0} | all-to-all | bytes 524288 | tf_op jit(solution)/shard_map/sum_heads/all_to_all | solution.py:294
  88.3 0.6 reduce_sum.12
  (1 shorter events, 0.0 us)
Async XLA Ops:
  2.1 14.1 %copy-start.2 = (bf16[4,512,1,128]{3,1,2,0:T(8,128)(2,1)S(1)}, bf16[4,512,1,128]{3,1,2,0:T(8,128)(2,1)}, u32[]{:S(2)}) copy-start(bf16[4,512,1,128]{3,1,2,0:T(8,128)(2,1)} %param.11) | copy-start | bytes 1572868
  2.1 17.5 %all-to-all-start = ((bf16[16,64,128]{2,1,0:T(8,128)(2,1)}), bf16[16,64,128]{2,1,0:T(8,128)(2,1)S(1)}, u32[]{:S(2)}, u32[]{:S(2)}) async-start(bf16[16,64,128]{2,1,0:T(8,128)(2,1)} %broadcast_in_dim.8), calls=%async_computation | async-start | bytes 524288 | tf_op jit(solution)/shard_map/gather_queries/all_to_all | solution.py:205
  11.8 4.4 %copy-start.1 = (bf16[4,512,1,128]{3,1,2,0:T(8,128)(2,1)S(1)}, bf16[4,512,1,128]{3,1,2,0:T(8,128)(2,1)}, u32[]{:S(2)}) copy-start(bf16[4,512,1,128]{3,1,2,0:T(8,128)(2,1)} %param.10) | copy-start | bytes 1572868
  11.8 4.4 %copy-start.3 = (bf16[4,16,128]{2,1,0:T(8,128)(2,1)S(1)}, bf16[4,16,128]{2,1,0:T(8,128)(2,1)}, u32[]{:S(2)}) copy-start(bf16[4,16,128]{2,1,0:T(8,128)(2,1)} %param.7) | copy-start | bytes 49156
  12.9 14.1 %collective-permute-start = (bf16[768,256]{1,0:T(8,128)(2,1)S(1)}, bf16[768,256]{1,0:T(8,128)(2,1)S(1)}, u32[]{:S(2)}, u32[]{:S(2)}) collective-permute-start(bf16[768,256]{1,0:T(8,128)(2,1)S(1)} %dynamic-slice_bitcast_fusion), channel_id=1, source_target_pairs={{0,32},{32,0},{1,33},{33,1},{2,34},{34,2},{3,35},{35,3},{4,36},{36... | collective-permute-start | bytes 1179656 | tf_op jit(solution)/shard_map/swap_weight/ppermute | solution.py:211
  16.2 0.7 copy-start.4
  16.2 3.4 %copy-start.5 = (bf16[4096,1,128]{2,0,1:T(8,128)(2,1)S(1)}, bf16[4096,1,128]{2,0,1:T(8,128)(2,1)}, u32[]{:S(2)}) copy-start(bf16[4096,1,128]{2,0,1:T(8,128)(2,1)} %param.8) | copy-start | bytes 3145732
  19.6 13.6 %copy-start = (bf16[2048,256]{1,0:T(8,128)(2,1)S(1)}, bf16[2048,256]{1,0:T(8,128)(2,1)}, u32[]{:S(2)}) copy-start(bf16[2048,256]{1,0:T(8,128)(2,1)} %weight_ref.1) | copy-start | bytes 3145732
  27.0 15.0 %all-to-all-start.1 = ((bf16[16,72,128]{2,1,0:T(8,128)(2,1)}), bf16[16,72,128]{2,1,0:T(8,128)(2,1)S(1)}, u32[]{:S(2)}, u32[]{:S(2)}) async-start(bf16[16,72,128]{2,1,0:T(8,128)(2,1)} %prompt_attention.1), calls=%async_computation.1 | async-start | bytes 589824 | tf_op jit(solution)/shard_map/return_partials/all_to_all | solution.py:262
  33.2 9.2 %collective-permute-start.1 = (bf16[256,256]{1,0:T(8,128)(2,1)S(1)}, bf16[256,256]{1,0:T(8,128)(2,1)S(1)}, u32[]{:S(2)}, u32[]{:S(2)}) collective-permute-start(bf16[256,256]{1,0:T(8,128)(2,1)S(1)} %dynamic-slice_bitcast_fusion.1), channel_id=1, source_target_pairs={{0,32},{32,0},{1,33},{33,1},{2,34},{34,2},{3,35},{35,3},{4,36},{36... | collective-permute-start | bytes 393224 | tf_op jit(solution)/shard_map/swap_weight/ppermute | solution.py:211

commit v7 on v6

--- a/solution.py
+++ b/solution.py
@@ -15,7 +15,7 @@
 KVH = ("x", "core")
 REP = ("z4", "z2")
 CTX_ORDER = ("zl", "y4", "y1", "y2")
-ALL_ORDER = ("y4", "y2", "y1", "z4", "z2", "zl")
+ALL_ORDER = ("y4", "y1", "y2", "z4", "z2", "zl")
 VMEM = pl.BlockSpec(memory_space=pltpu.VMEM)
 HBM = pl.BlockSpec(memory_space=pltpu.HBM)
 SMEM = pl.BlockSpec(memory_space=pltpu.SMEM)
@@ -226,7 +226,7 @@
                 transcendentals=conts * slots * head_dim,
             ),
         )(
-            suffix_len,
+            pltpu.with_memory_space_constraint(suffix_len, pltpu.HBM),
             query_rows,
             suffix_keys.reshape(conts * slots, head_dim),
             suffix_values.reshape(conts * slots, head_dim),

time: 89.4 us -> 89.1 us (level)
  no operation moved by 1% of the time
where the time goes in v7:
time: 89.1 us; the launch traced here: 88.4 us
  blocking collectives  44.7 us (50%)
  starting transfers between devices  22.4 us (25%)
  Pallas kernels  10.2 us (11%)
  waiting for transfers between devices  6.98 us (8%)
  local copies, waits for them, and re-layouts  2.66 us (3%)
    all_to_all x1, blocking collectives, body(): everyone = lax.all_to_all(copies, ALL_ORDER, 0, 0, tiled=False)  28.6 us
    all_to_all x1, blocking collectives, body(): parts = lax.all_to_all(terms, KVH + ('zl',), 0, 0, tiled=False)  16.1 us
    all_to_all x1, starting transfers between devices, body(): visiting = lax.all_to_all(copies, CTX_ORDER, 0, 0, tiled=False)  9.69 us
    pallas_call x1, Pallas kernels, body(): pl.pallas_call(prompt_kernel, in_specs=[VMEM, VMEM, HBM], out_specs=VMEM,...  7.35 us
    ppermute x2, starting transfers between devices, body(): lax.ppermute(part, 'zl', [(0, 1), (1, 0)])  6.55 us
    all_to_all x1, starting transfers between devices, body(): back = lax.all_to_all(sent, CTX_ORDER, 0, 0, tiled=False)  6.2 us
    all_to_all x1, waiting for transfers between devices, body(): back = lax.all_to_all(sent, CTX_ORDER, 0, 0, tiled=False)  5.42 us
  transfers between devices with their start and end apart: 4, of which 2 were waited for; matrix products, arithmetic and copies ran while one was open for 1% of the time, Pallas kernels for 11%

profile of v7, /device:TPU:1, one launch (start us, length us, event | category | flops | bytes accessed | tf_op | source)
XLA Modules:
  0.0 88.4 jit_solution(9965648969942257350)
XLA Ops:
  0.6 1.5 %broadcast_in_dim.8 = bf16[16,64,128]{2,1,0:T(8,128)(2,1)} broadcast(bf16[64,128]{1,0:T(8,128)(2,1)} %bitcast.17), dimensions={1,2} | broadcast | bytes 278528 | tf_op jit(solution)/shard_map/gather_queries/broadcast_in_dim | solution.py:204
  2.1 0.0 copy-start.2
  2.1 9.7 %all-to-all-start = ((bf16[16,64,128]{2,1,0:T(8,128)(2,1)}), bf16[16,64,128]{2,1,0:T(8,128)(2,1)S(1)}, u32[]{:S(2)}, u32[]{:S(2)}) async-start(bf16[16,64,128]{2,1,0:T(8,128)(2,1)} %broadcast_in_dim.8), calls=%async_computation | async-start | bytes 524288 | tf_op jit(solution)/shard_map/gather_queries/all_to_all | solution.py:205
  11.8 0.0 copy-start.1
  11.8 0.0 copy-start.3
  11.8 0.0 copy-start.4
  11.9 1.1 %dynamic-slice_bitcast_fusion = bf16[768,256]{1,0:T(8,128)(2,1)S(1)} fusion(bf16[2,1024,256]{2,1,0:T(8,128)(2,1)} %bitcast.13, s32[]{:T(128)S(6)} %select_n.4), kind=kLoop, calls=%fused_computation | loop fusion | bytes 786436 | tf_op jit(solution)/shard_map/swap_weight/slice | solution.py:211
  13.0 3.3 %collective-permute-start = (bf16[768,256]{1,0:T(8,128)(2,1)S(1)}, bf16[768,256]{1,0:T(8,128)(2,1)S(1)}, u32[]{:S(2)}, u32[]{:S(2)}) collective-permute-start(bf16[768,256]{1,0:T(8,128)(2,1)S(1)} %dynamic-slice_bitcast_fusion), channel_id=1, source_target_pairs={{0,32},{32,0},{1,33},{33,1},{2,34},{34,2},{3,35},{35,3},{4,36},{36... | collective-permute-start | bytes 1179656 | tf_op jit(solution)/shard_map/swap_weight/ppermute | solution.py:211
  16.3 0.0 copy-done.2
  16.3 0.0 copy-done.1
  16.3 0.0 copy-done.3
  16.3 1.7 %suffix_attention.1 = (f32[64,128]{1,0:T(8,128)S(1)}, f32[8,128]{1,0:T(8,128)S(1)}) custom-call(s32[4]{0:T(128)} %len_ref.1, bf16[64,128]{1,0:T(8,128)(2,1)S(1)} %bitcast.18, bf16[2048,128]{1,0:T(8,128)(2,1)S(1)} %bitcast.15, bf16[2048,128]{1,0:T(8,128)(2,1)S(1)} %bitcast.16), custom_call_target="tpu_custom_call" | custom-call | flops 134217728 | bytes 1048576 | tf_op jit(solution)/shard_map/suffix_attention/pallas_call | solution.py:214
  18.0 1.6 %all-to-all-done.query_ref = bf16[16,64,128]{2,1,0:T(8,128)(2,1)S(1)} async-done(((bf16[16,64,128]{2,1,0:T(8,128)(2,1)}), bf16[16,64,128]{2,1,0:T(8,128)(2,1)S(1)}, u32[]{:S(2)}, u32[]{:S(2)}) %all-to-all-start) | async-done | bytes 262176 | tf_op jit(solution)/shard_map/gather_queries/all_to_all | solution.py:205
  19.6 0.0 copy-done.4
  19.6 0.0 copy-start
  19.6 7.3 %prompt_attention.1 = bf16[16,72,128]{2,1,0:T(8,128)(2,1)} custom-call(bf16[16,64,128]{2,1,0:T(8,128)(2,1)S(1)} %all-to-all-done.query_ref, bf16[4096,128]{1,0:T(8,128)(2,1)S(1)} %bitcast.19, bf16[4096,128]{1,0:T(8,128)(2,1)} %bitcast.20), custom_call_target="tpu_custom_call" | custom-call | flops 2147483648 | bytes 2097152 | tf_op jit(solution)/shard_map/prompt_attention/pallas_call | solution.py:238
  27.0 0.0 collective-permute-done.upper_ref
  27.0 6.2 %all-to-all-start.1 = ((bf16[16,72,128]{2,1,0:T(8,128)(2,1)}), bf16[16,72,128]{2,1,0:T(8,128)(2,1)S(1)}, u32[]{:S(2)}, u32[]{:S(2)}) async-start(bf16[16,72,128]{2,1,0:T(8,128)(2,1)} %prompt_attention.1), calls=%async_computation.1 | async-start | bytes 589824 | tf_op jit(solution)/shard_map/return_partials/all_to_all | solution.py:262
  33.2 0.0 copy-done
  33.2 3.3 %collective-permute-start.1 = (bf16[256,256]{1,0:T(8,128)(2,1)S(1)}, bf16[256,256]{1,0:T(8,128)(2,1)S(1)}, u32[]{:S(2)}, u32[]{:S(2)}) collective-permute-start(bf16[256,256]{1,0:T(8,128)(2,1)S(1)} %dynamic-slice_bitcast_fusion.1), channel_id=1, source_target_pairs={{0,32},{32,0},{1,33},{33,1},{2,34},{34,2},{3,35},{35,3},{4,36},{36... | collective-permute-start | bytes 393224 | tf_op jit(solution)/shard_map/swap_weight/ppermute | solution.py:211
  36.5 5.4 %all-to-all-done.1.back_ref = bf16[16,72,128]{2,1,0:T(8,128)(2,1)S(1)} async-done(((bf16[16,72,128]{2,1,0:T(8,128)(2,1)}), bf16[16,72,128]{2,1,0:T(8,128)(2,1)S(1)}, u32[]{:S(2)}, u32[]{:S(2)}) %all-to-all-start.1) | async-done | bytes 294944 | tf_op jit(solution)/shard_map/return_partials/all_to_all | solution.py:262
  41.9 0.4 combine.1
  42.4 0.0 collective-permute-done.1.lower_ref
  42.4 28.6 %all_to_all.20.block_ref = bf16[64,32,128]{2,1,0:T(8,128)(2,1)S(1)} all-to-all(bf16[64,32,128]{2,1,0:T(8,128)(2,1)S(1)} %get-tuple-element.22), channel_id=1, replica_groups=mesh['y4'=2,'y2'=2,'y1'=2,'zl'=2,'x'=4,'core'=2,'z4'=2,'z2'=2] {'y4','y1..., dimensions={0} | all-to-all | bytes 1048576 | tf_op jit(solution)/shard_map/gather_attended/all_to_all | solution.py:277
  71.0 0.6 project.1
  71.6 16.1 %all_to_all.21 = bf16[16,32,256]{2,1,0:T(8,128)(2,1)S(1)} all-to-all(bf16[16,32,256]{2,1,0:T(8,128)(2,1)S(1)} %get-tuple-element.27), channel_id=1, replica_groups=mesh['y4'=2,'y2'=2,'y1'=2,'zl'=2,'x'=4,'core'=2,'z4'=2,'z2'=2] {'x','cor..., dimensions={0} | all-to-all | bytes 524288 | tf_op jit(solution)/shard_map/sum_heads/all_to_all | solution.py:294
  87.7 0.6 reduce_sum.12
  (1 shorter events, 0.0 us)
Async XLA Ops:
  2.1 14.2 %copy-start.2 = (bf16[4,512,1,128]{3,1,2,0:T(8,128)(2,1)S(1)}, bf16[4,512,1,128]{3,1,2,0:T(8,128)(2,1)}, u32[]{:S(2)}) copy-start(bf16[4,512,1,128]{3,1,2,0:T(8,128)(2,1)} %param.11) | copy-start | bytes 1572868
  2.1 17.5 %all-to-all-start = ((bf16[16,64,128]{2,1,0:T(8,128)(2,1)}), bf16[16,64,128]{2,1,0:T(8,128)(2,1)S(1)}, u32[]{:S(2)}, u32[]{:S(2)}) async-start(bf16[16,64,128]{2,1,0:T(8,128)(2,1)} %broadcast_in_dim.8), calls=%async_computation | async-start | bytes 524288 | tf_op jit(solution)/shard_map/gather_queries/all_to_all | solution.py:205
  11.8 4.5 %copy-start.1 = (bf16[4,512,1,128]{3,1,2,0:T(8,128)(2,1)S(1)}, bf16[4,512,1,128]{3,1,2,0:T(8,128)(2,1)}, u32[]{:S(2)}) copy-start(bf16[4,512,1,128]{3,1,2,0:T(8,128)(2,1)} %param.10) | copy-start | bytes 1572868
  11.8 4.5 %copy-start.3 = (bf16[4,16,128]{2,1,0:T(8,128)(2,1)S(1)}, bf16[4,16,128]{2,1,0:T(8,128)(2,1)}, u32[]{:S(2)}) copy-start(bf16[4,16,128]{2,1,0:T(8,128)(2,1)} %param.7) | copy-start | bytes 49156
  11.8 7.8 %copy-start.4 = (bf16[4096,1,128]{2,0,1:T(8,128)(2,1)S(1)}, bf16[4096,1,128]{2,0,1:T(8,128)(2,1)}, u32[]{:S(2)}) copy-start(bf16[4096,1,128]{2,0,1:T(8,128)(2,1)} %param.8) | copy-start | bytes 3145732
  13.0 14.0 %collective-permute-start = (bf16[768,256]{1,0:T(8,128)(2,1)S(1)}, bf16[768,256]{1,0:T(8,128)(2,1)S(1)}, u32[]{:S(2)}, u32[]{:S(2)}) collective-permute-start(bf16[768,256]{1,0:T(8,128)(2,1)S(1)} %dynamic-slice_bitcast_fusion), channel_id=1, source_target_pairs={{0,32},{32,0},{1,33},{33,1},{2,34},{34,2},{3,35},{35,3},{4,36},{36... | collective-permute-start | bytes 1179656 | tf_op jit(solution)/shard_map/swap_weight/ppermute | solution.py:211
  19.6 13.6 %copy-start = (bf16[2048,256]{1,0:T(8,128)(2,1)S(1)}, bf16[2048,256]{1,0:T(8,128)(2,1)}, u32[]{:S(2)}) copy-start(bf16[2048,256]{1,0:T(8,128)(2,1)} %weight_ref.1) | copy-start | bytes 3145732
  27.0 15.0 %all-to-all-start.1 = ((bf16[16,72,128]{2,1,0:T(8,128)(2,1)}), bf16[16,72,128]{2,1,0:T(8,128)(2,1)S(1)}, u32[]{:S(2)}, u32[]{:S(2)}) async-start(bf16[16,72,128]{2,1,0:T(8,128)(2,1)} %prompt_attention.1), calls=%async_computation.1 | async-start | bytes 589824 | tf_op jit(solution)/shard_map/return_partials/all_to_all | solution.py:262
  33.2 9.2 %collective-permute-start.1 = (bf16[256,256]{1,0:T(8,128)(2,1)S(1)}, bf16[256,256]{1,0:T(8,128)(2,1)S(1)}, u32[]{:S(2)}, u32[]{:S(2)}) collective-permute-start(bf16[256,256]{1,0:T(8,128)(2,1)S(1)} %dynamic-slice_bitcast_fusion.1), channel_id=1, source_target_pairs={{0,32},{32,0},{1,33},{33,1},{2,34},{34,2},{3,35},{35,3},{4,36},{36... | collective-permute-start | bytes 393224 | tf_op jit(solution)/shard_map/swap_weight/ppermute | solution.py:211

commit v8 on v6

--- a/solution.py
+++ b/solution.py
@@ -185,6 +185,13 @@
     home_copy.wait()
 
 
+def sum_kernel(part_ref, out_ref):
+    total = part_ref[0].astype(jnp.float32)
+    for part in range(1, part_ref.shape[0]):
+        total += part_ref[part].astype(jnp.float32)
+    out_ref[...] = total.astype(out_ref.dtype)
+
+
 def body(queries, prompt_keys, prompt_values, suffix_keys, suffix_values, suffix_len, out_weight):
     conts, heads, head_dim = queries.shape
     rows = conts * heads
@@ -292,7 +299,13 @@
         )(half.reshape(1), everyone, out_weight, taken[0], taken[1], attended)
     with jax.named_scope("sum_heads"):
         parts = lax.all_to_all(terms, KVH + ("zl",), 0, 0, tiled=False)
-        projected = jnp.sum(parts.astype(jnp.float32), axis=0).astype(jnp.bfloat16)
+        projected = pl.pallas_call(
+            sum_kernel,
+            in_specs=[VMEM],
+            out_specs=VMEM,
+            out_shape=jax.ShapeDtypeStruct(parts.shape[1:], jnp.bfloat16),
+            compiler_params=small,
+        )(parts)
     return (attended.reshape(conts, heads, head_dim), projected)
 
 

time: 89.4 us -> 89.4 us (level)
  no operation moved by 1% of the time
where the time goes in v8:
time: 89.4 us; the launch traced here: 88.9 us
  blocking collectives  45.2 us (51%)
  starting transfers between devices  22.4 us (25%)
  Pallas kernels  10.7 us (12%)
  waiting for transfers between devices  6.55 us (7%)
  local copies, waits for them, and re-layouts  3.21 us (4%)
    all_to_all x1, blocking collectives, body(): everyone = lax.all_to_all(copies, ALL_ORDER, 0, 0, tiled=False)  28.3 us
    all_to_all x1, blocking collectives, body(): parts = lax.all_to_all(terms, KVH + ('zl',), 0, 0, tiled=False)  16.9 us
    all_to_all x1, starting transfers between devices, body(): visiting = lax.all_to_all(copies, CTX_ORDER, 0, 0, tiled=False)  9.69 us
    pallas_call x1, Pallas kernels, body(): pl.pallas_call(prompt_kernel, in_specs=[VMEM, VMEM, HBM], out_specs=VMEM,...  7.34 us
    ppermute x2, starting transfers between devices, body(): lax.ppermute(part, 'zl', [(0, 1), (1, 0)])  6.55 us
    all_to_all x1, starting transfers between devices, body(): back = lax.all_to_all(sent, CTX_ORDER, 0, 0, tiled=False)  6.2 us
    all_to_all x1, waiting for transfers between devices, body(): back = lax.all_to_all(sent, CTX_ORDER, 0, 0, tiled=False)  5.42 us
  transfers between devices with their start and end apart: 4, of which 2 were waited for; matrix products, arithmetic and copies ran while one was open for 1% of the time, Pallas kernels for 11%

profile of v8, /device:TPU:1, one launch (start us, length us, event | category | flops | bytes accessed | tf_op | source)
XLA Modules:
  0.0 88.9 jit_solution(14528082210831908359)
XLA Ops:
  0.6 1.5 %broadcast_in_dim.8 = bf16[16,64,128]{2,1,0:T(8,128)(2,1)} broadcast(bf16[64,128]{1,0:T(8,128)(2,1)} %bitcast.17), dimensions={1,2} | broadcast | bytes 278528 | tf_op jit(solution)/shard_map/gather_queries/broadcast_in_dim | solution.py:211
  2.1 0.0 copy-start.2
  2.1 9.7 %all-to-all-start = ((bf16[16,64,128]{2,1,0:T(8,128)(2,1)}), bf16[16,64,128]{2,1,0:T(8,128)(2,1)S(1)}, u32[]{:S(2)}, u32[]{:S(2)}) async-start(bf16[16,64,128]{2,1,0:T(8,128)(2,1)} %broadcast_in_dim.8), calls=%async_computation | async-start | bytes 524288 | tf_op jit(solution)/shard_map/gather_queries/all_to_all | solution.py:212
  11.8 0.0 copy-start.1
  11.8 0.0 copy-start.3
  11.8 1.1 %dynamic-slice_bitcast_fusion = bf16[768,256]{1,0:T(8,128)(2,1)S(1)} fusion(bf16[2,1024,256]{2,1,0:T(8,128)(2,1)} %bitcast.13, s32[]{:T(128)S(6)} %select_n.4), kind=kLoop, calls=%fused_computation | loop fusion | bytes 786436 | tf_op jit(solution)/shard_map/swap_weight/slice | solution.py:218
  12.9 3.3 %collective-permute-start = (bf16[768,256]{1,0:T(8,128)(2,1)S(1)}, bf16[768,256]{1,0:T(8,128)(2,1)S(1)}, u32[]{:S(2)}, u32[]{:S(2)}) collective-permute-start(bf16[768,256]{1,0:T(8,128)(2,1)S(1)} %dynamic-slice_bitcast_fusion), channel_id=1, source_target_pairs={{0,32},{32,0},{1,33},{33,1},{2,34},{34,2},{3,35},{35,3},{4,36},{36... | collective-permute-start | bytes 1179656 | tf_op jit(solution)/shard_map/swap_weight/ppermute | solution.py:218
  16.2 0.0 copy-start.4
  16.2 0.0 copy-start.5
  16.2 0.0 copy-done.2
  16.2 0.0 copy-done.1
  16.2 0.0 copy-done.3
  16.3 0.6 copy-done.4
  16.9 1.6 %suffix_attention.1 = (f32[64,128]{1,0:T(8,128)S(1)}, f32[8,128]{1,0:T(8,128)S(1)}) custom-call(s32[4]{0:T(128)S(1)} %copy-done.4, bf16[64,128]{1,0:T(8,128)(2,1)S(1)} %bitcast.18, bf16[2048,128]{1,0:T(8,128)(2,1)S(1)} %bitcast.15, bf16[2048,128]{1,0:T(8,128)(2,1)S(1)} %bitcast.16), custom_call_target="tpu_custom_call" | custom-call | flops 134217728 | bytes 1048576 | tf_op jit(solution)/shard_map/suffix_attention/pallas_call | solution.py:221
  18.5 1.1 %all-to-all-done.query_ref = bf16[16,64,128]{2,1,0:T(8,128)(2,1)S(1)} async-done(((bf16[16,64,128]{2,1,0:T(8,128)(2,1)}), bf16[16,64,128]{2,1,0:T(8,128)(2,1)S(1)}, u32[]{:S(2)}, u32[]{:S(2)}) %all-to-all-start) | async-done | bytes 262176 | tf_op jit(solution)/shard_map/gather_queries/all_to_all | solution.py:212
  19.6 0.0 copy-done.5
  19.6 0.0 copy-start
  19.6 7.3 %prompt_attention.1 = bf16[16,72,128]{2,1,0:T(8,128)(2,1)} custom-call(bf16[16,64,128]{2,1,0:T(8,128)(2,1)S(1)} %all-to-all-done.query_ref, bf16[4096,128]{1,0:T(8,128)(2,1)S(1)} %bitcast.19, bf16[4096,128]{1,0:T(8,128)(2,1)} %bitcast.20), custom_call_target="tpu_custom_call" | custom-call | flops 2147483648 | bytes 2097152 | tf_op jit(solution)/shard_map/prompt_attention/pallas_call | solution.py:245
  27.0 0.0 collective-permute-done.upper_ref
  27.0 6.2 %all-to-all-start.1 = ((bf16[16,72,128]{2,1,0:T(8,128)(2,1)}), bf16[16,72,128]{2,1,0:T(8,128)(2,1)S(1)}, u32[]{:S(2)}, u32[]{:S(2)}) async-start(bf16[16,72,128]{2,1,0:T(8,128)(2,1)} %prompt_attention.1), calls=%async_computation.1 | async-start | bytes 589824 | tf_op jit(solution)/shard_map/return_partials/all_to_all | solution.py:269
  33.2 0.0 copy-done
  33.2 3.3 %collective-permute-start.1 = (bf16[256,256]{1,0:T(8,128)(2,1)S(1)}, bf16[256,256]{1,0:T(8,128)(2,1)S(1)}, u32[]{:S(2)}, u32[]{:S(2)}) collective-permute-start(bf16[256,256]{1,0:T(8,128)(2,1)S(1)} %dynamic-slice_bitcast_fusion.1), channel_id=1, source_target_pairs={{0,32},{32,0},{1,33},{33,1},{2,34},{34,2},{3,35},{35,3},{4,36},{36... | collective-permute-start | bytes 393224 | tf_op jit(solution)/shard_map/swap_weight/ppermute | solution.py:218
  36.5 5.4 %all-to-all-done.1.back_ref = bf16[16,72,128]{2,1,0:T(8,128)(2,1)S(1)} async-done(((bf16[16,72,128]{2,1,0:T(8,128)(2,1)}), bf16[16,72,128]{2,1,0:T(8,128)(2,1)S(1)}, u32[]{:S(2)}, u32[]{:S(2)}) %all-to-all-start.1) | async-done | bytes 294944 | tf_op jit(solution)/shard_map/return_partials/all_to_all | solution.py:269
  41.9 0.4 combine.1
  42.4 0.0 collective-permute-done.1.lower_ref
  42.4 28.3 %all_to_all.20.block_ref = bf16[64,32,128]{2,1,0:T(8,128)(2,1)S(1)} all-to-all(bf16[64,32,128]{2,1,0:T(8,128)(2,1)S(1)} %get-tuple-element.22), channel_id=1, replica_groups=mesh['y4'=2,'y2'=2,'y1'=2,'zl'=2,'x'=4,'core'=2,'z4'=2,'z2'=2] {'y4','y2..., dimensions={0} | all-to-all | bytes 1048576 | tf_op jit(solution)/shard_map/gather_attended/all_to_all | solution.py:284
  70.7 0.6 project.1
  71.4 16.9 %all_to_all.21.part_ref = bf16[16,32,256]{2,1,0:T(8,128)(2,1)S(1)} all-to-all(bf16[16,32,256]{2,1,0:T(8,128)(2,1)S(1)} %get-tuple-element.27), channel_id=1, replica_groups=mesh['y4'=2,'y2'=2,'y1'=2,'zl'=2,'x'=4,'core'=2,'z4'=2,'z2'=2] {'x','cor..., dimensions={0} | all-to-all | bytes 524288 | tf_op jit(solution)/shard_map/sum_heads/all_to_all | solution.py:301
  88.3 0.6 sum_heads.1
  (1 shorter events, 0.0 us)
Async XLA Ops:
  2.1 14.1 %copy-start.2 = (bf16[4,512,1,128]{3,1,2,0:T(8,128)(2,1)S(1)}, bf16[4,512,1,128]{3,1,2,0:T(8,128)(2,1)}, u32[]{:S(2)}) copy-start(bf16[4,512,1,128]{3,1,2,0:T(8,128)(2,1)} %param.11) | copy-start | bytes 1572868
  2.1 17.5 %all-to-all-start = ((bf16[16,64,128]{2,1,0:T(8,128)(2,1)}), bf16[16,64,128]{2,1,0:T(8,128)(2,1)S(1)}, u32[]{:S(2)}, u32[]{:S(2)}) async-start(bf16[16,64,128]{2,1,0:T(8,128)(2,1)} %broadcast_in_dim.8), calls=%async_computation | async-start | bytes 524288 | tf_op jit(solution)/shard_map/gather_queries/all_to_all | solution.py:212
  11.8 4.4 %copy-start.1 = (bf16[4,512,1,128]{3,1,2,0:T(8,128)(2,1)S(1)}, bf16[4,512,1,128]{3,1,2,0:T(8,128)(2,1)}, u32[]{:S(2)}) copy-start(bf16[4,512,1,128]{3,1,2,0:T(8,128)(2,1)} %param.10) | copy-start | bytes 1572868
  11.8 4.4 %copy-start.3 = (bf16[4,16,128]{2,1,0:T(8,128)(2,1)S(1)}, bf16[4,16,128]{2,1,0:T(8,128)(2,1)}, u32[]{:S(2)}) copy-start(bf16[4,16,128]{2,1,0:T(8,128)(2,1)} %param.7) | copy-start | bytes 49156
  12.9 14.0 %collective-permute-start = (bf16[768,256]{1,0:T(8,128)(2,1)S(1)}, bf16[768,256]{1,0:T(8,128)(2,1)S(1)}, u32[]{:S(2)}, u32[]{:S(2)}) collective-permute-start(bf16[768,256]{1,0:T(8,128)(2,1)S(1)} %dynamic-slice_bitcast_fusion), channel_id=1, source_target_pairs={{0,32},{32,0},{1,33},{33,1},{2,34},{34,2},{3,35},{35,3},{4,36},{36... | collective-permute-start | bytes 1179656 | tf_op jit(solution)/shard_map/swap_weight/ppermute | solution.py:218
  16.2 0.7 copy-start.4
  16.2 3.4 %copy-start.5 = (bf16[4096,1,128]{2,0,1:T(8,128)(2,1)S(1)}, bf16[4096,1,128]{2,0,1:T(8,128)(2,1)}, u32[]{:S(2)}) copy-start(bf16[4096,1,128]{2,0,1:T(8,128)(2,1)} %param.8) | copy-start | bytes 3145732
  19.6 13.6 %copy-start = (bf16[2048,256]{1,0:T(8,128)(2,1)S(1)}, bf16[2048,256]{1,0:T(8,128)(2,1)}, u32[]{:S(2)}) copy-start(bf16[2048,256]{1,0:T(8,128)(2,1)} %weight_ref.1) | copy-start | bytes 3145732
  27.0 15.0 %all-to-all-start.1 = ((bf16[16,72,128]{2,1,0:T(8,128)(2,1)}), bf16[16,72,128]{2,1,0:T(8,128)(2,1)S(1)}, u32[]{:S(2)}, u32[]{:S(2)}) async-start(bf16[16,72,128]{2,1,0:T(8,128)(2,1)} %prompt_attention.1), calls=%async_computation.1 | async-start | bytes 589824 | tf_op jit(solution)/shard_map/return_partials/all_to_all | solution.py:269
  33.2 9.2 %collective-permute-start.1 = (bf16[256,256]{1,0:T(8,128)(2,1)S(1)}, bf16[256,256]{1,0:T(8,128)(2,1)S(1)}, u32[]{:S(2)}, u32[]{:S(2)}) collective-permute-start(bf16[256,256]{1,0:T(8,128)(2,1)S(1)} %dynamic-slice_bitcast_fusion.1), channel_id=1, source_target_pairs={{0,32},{32,0},{1,33},{33,1},{2,34},{34,2},{3,35},{35,3},{4,36},{36... | collective-permute-start | bytes 393224 | tf_op jit(solution)/shard_map/swap_weight/ppermute | solution.py:218
